TPU v7x, 32 devices: a whole 2x2x4 slice. The times are simulated.
32 devices in a mesh: dp: 16 (over z, y, x), tensor: 2 (over core).
Axes of the slice: x: 2, y: 2, z: 4, core: 2. Of those that a mesh axis runs over, the one named last changes fastest.
Arguments:
- tokens: bfloat16 [32768, 768], P('dp')
- cotangent: bfloat16 [32768, 768], P('dp'), may hold values from -6 to 6
- pair_lengths: int32 [32, 8], P('dp'), may hold values from 1 to 1017, as said below
- mat_master: float32 [768, 96, 96], P(('dp', 'tensor'))
- mat_left: float32 [768, 96, 96], P(('dp', 'tensor')), as said below
- mat_right: float32 [768, 96, 96], P(('dp', 'tensor')), as said below
- root_left: float32 [768, 96, 96], P(('dp', 'tensor'))
- root_right: float32 [768, 96, 96], P(('dp', 'tensor'))
- vec_master: float32 [9216], P(('dp', 'tensor'))
- vec_second: float32 [9216], P(('dp', 'tensor'))
Outputs:
- block_out: bfloat16 [32768, 768], P('dp')
- input_grad: float32 [32768, 768], P('dp')
- mat_grads: float32 [768, 96, 96], P(('dp', 'tensor'))
- mat_left_new: float32 [768, 96, 96], P(('dp', 'tensor'))
- mat_right_new: float32 [768, 96, 96], P(('dp', 'tensor'))
- mat_new: float32 [768, 96, 96], P(('dp', 'tensor'))
- vec_grads: float32 [9216], P(('dp', 'tensor'))
- vec_second_new: float32 [9216], P(('dp', 'tensor'))
- vec_new: float32 [9216], P(('dp', 'tensor'))
- stream_rms: float32 [3], replicated
Inputs may be any that keep to these rules, and one draw needn't show every extreme that they name: `pair_lengths`: in each row the 8 lengths add up to at most 1024; the positions after them are padding. `mat_left`: each block is symmetric. `mat_right`: each block is symmetric.
All inputs are finite; a program needn't handle non-finite values.
Results may differ from a plain program's by a relative error of at most 0.017.
Values may be sent and summed in bfloat16 or wider, within the bound.
A program may use at most 192 MiB of HBM per device.

v0:
```python
from functools import partial
import math

import jax
import jax.numpy as jnp
from jax import lax
from jax.sharding import PartitionSpec as P

HD = 64


LN_EPS = 1e-12
NEG_FILL = -1e30
DECAY = 0.5
STEP_RATE = 1.0
VEC_RATE = 0.1
VEC_EPS = 1e-08
INV_ROOT_TWO = 1.0 / math.sqrt(2.0)
INV_ROOT_TWO_PI = 1.0 / math.sqrt(2.0 * math.pi)
HIGHEST = lax.Precision.HIGHEST


def unblock(blocks, grid_rows, grid_cols):
    edge = blocks.shape[-1]
    return (
        blocks.reshape(grid_rows, grid_cols, edge, edge)
        .transpose(0, 2, 1, 3)
        .reshape(grid_rows * edge, grid_cols * edge)
    )


def to_blocks(matrix, edge):
    grid_rows = matrix.shape[0] // edge
    grid_cols = matrix.shape[1] // edge
    return (
        matrix.reshape(grid_rows, edge, grid_cols, edge)
        .transpose(0, 2, 1, 3)
        .reshape(grid_rows * grid_cols, edge, edge)
    )


def pair_index(lengths, seq_len):
    ends = jnp.cumsum(lengths, axis=-1)
    places = lax.broadcasted_iota(jnp.int32, (lengths.shape[0], seq_len, 1), 1)
    return jnp.sum((places >= ends[:, None, :]).astype(jnp.int32), axis=-1)


def layer_norm(residual, gain, shift):
    centred = residual - jnp.mean(residual, axis=-1, keepdims=True)
    inverse_spread = lax.rsqrt(jnp.mean(centred * centred, axis=-1, keepdims=True) + LN_EPS)
    normal = centred * inverse_spread
    return (normal * gain + shift, normal, inverse_spread)


def norm_back(grad_output, normal, inverse_spread, gain):
    scaled = grad_output * gain
    grad_input = inverse_spread * (
        scaled
        - jnp.mean(scaled, axis=-1, keepdims=True)
        - normal * jnp.mean(scaled * normal, axis=-1, keepdims=True)
    )
    return (grad_input, jnp.sum(grad_output * normal, axis=0), jnp.sum(grad_output, axis=0))


def gelu_slope(pre_act):
    return (
        0.5 * (1.0 + lax.erf(pre_act * INV_ROOT_TWO))
        + pre_act * jnp.exp(-0.5 * pre_act * pre_act) * INV_ROOT_TWO_PI
    )


def block_scores(query_blk, key_row, pair_query, pair_key, pair_count, scale):
    scores = (
        jnp.einsum("qhd,khd->hqk", query_blk, key_row, preferred_element_type=jnp.float32) * scale
    )
    allowed = (pair_query[:, None] == pair_key[None, :]) & (pair_key[None, :] < pair_count)
    return (jnp.where(allowed[None], scores, NEG_FILL), allowed)


def block_forward(operand, pair_count, scale):
    query_blk, key_row, value_row, pair_query, pair_key = operand
    masked, allowed = block_scores(query_blk, key_row, pair_query, pair_key, pair_count, scale)
    top = jnp.max(masked, axis=-1, keepdims=True)
    weights = jnp.where(allowed[None], jnp.exp(masked - top), 0.0)
    total = jnp.maximum(jnp.sum(weights, axis=-1, keepdims=True), 0.5)
    probs_low = (weights / total).astype(jnp.bfloat16)
    context = jnp.einsum(
        "hqk,khd->qhd", probs_low, value_row, preferred_element_type=jnp.float32
    ).astype(jnp.bfloat16)
    return (context, top, total)


def block_backward(operand, pair_count, scale):
    query_blk, key_row, value_row, grad_blk, pair_query, pair_key, top, total = operand
    masked, allowed = block_scores(query_blk, key_row, pair_query, pair_key, pair_count, scale)
    probs = jnp.where(allowed[None], jnp.exp(masked - top), 0.0) / total
    probs_low = probs.astype(jnp.bfloat16)
    grad_probs = jnp.einsum("qhd,khd->hqk", grad_blk, value_row, preferred_element_type=jnp.float32)
    centre = jnp.sum(probs * grad_probs, axis=-1, keepdims=True)
    grad_scores = (probs * (grad_probs - centre)).astype(jnp.bfloat16)
    grad_query = (
        jnp.einsum("hqk,khd->qhd", grad_scores, key_row, preferred_element_type=jnp.float32) * scale
    )
    grad_key = (
        jnp.einsum("hqk,qhd->khd", grad_scores, query_blk, preferred_element_type=jnp.float32)
        * scale
    )
    grad_value = jnp.einsum("hqk,qhd->khd", probs_low, grad_blk, preferred_element_type=jnp.float32)
    return (grad_query, grad_key, grad_value)


def row_forward(items, pair_count, scale, width):
    query_row, key_row, value_row, pair_row = items
    contexts = []
    tops = []
    totals = []
    compute = partial(block_forward, pair_count=pair_count, scale=scale)
    for start in range(0, query_row.shape[0], width):
        pair_query = pair_row[start : start + width]
        operand = (query_row[start : start + width], key_row, value_row, pair_query, pair_row)
        context, top, total = compute(operand)
        contexts.append(context)
        tops.append(top)
        totals.append(total)
    return (jnp.concatenate(contexts, axis=0), jnp.stack(tops), jnp.stack(totals))


def row_backward(items, pair_count, scale, width):
    query_row, key_row, value_row, grad_row, pair_row, tops, totals = items
    grad_keys = jnp.zeros(key_row.shape, jnp.float32)
    grad_values = jnp.zeros(value_row.shape, jnp.float32)
    grad_queries = []
    compute = partial(block_backward, pair_count=pair_count, scale=scale)
    for index, start in enumerate(range(0, query_row.shape[0], width)):
        pair_query = pair_row[start : start + width]
        operand = (
            query_row[start : start + width],
            key_row,
            value_row,
            grad_row[start : start + width],
            pair_query,
            pair_row,
            tops[index],
            totals[index],
        )
        grad_query, grad_key, grad_value = compute(operand)
        grad_queries.append(grad_query)
        grad_keys = grad_keys + grad_key
        grad_values = grad_values + grad_value
    return (jnp.concatenate(grad_queries, axis=0), grad_keys, grad_values)


def body(
    tokens,
    cotangent,
    pair_lengths,
    mat_master,
    mat_left,
    mat_right,
    root_left,
    root_right,
    vec_master,
    vec_second,
):
    width = tokens.shape[1]
    half = width // 2
    heads_local = half // HD
    row_count = pair_lengths.shape[0]
    pair_count = pair_lengths.shape[1]
    seq_len = tokens.shape[0] // row_count
    block_width = min(512, seq_len)
    scale = HD ** (-0.5)
    edge = mat_master.shape[-1]
    own_index = lax.axis_index("tensor")
    local_blocks = mat_master.astype(jnp.bfloat16).reshape(3, -1, edge, edge)
    blocks = lax.all_gather(local_blocks, "dp", axis=1, tiled=True)
    kind_count = blocks.shape[1]
    quarter = kind_count // 4
    grid_model = width // edge
    grid_half = half // edge
    grid_hidden = kind_count // grid_model
    w_project = (
        blocks[0, : 3 * quarter]
        .reshape(3, grid_model, grid_half, edge, edge)
        .transpose(1, 3, 0, 2, 4)
        .reshape(width, 3 * half)
    )
    w_out = unblock(blocks[0, 3 * quarter :], grid_half, grid_model)
    w_up = unblock(blocks[1], grid_model, grid_hidden)
    w_down = unblock(blocks[2], grid_hidden, grid_model)
    shard = vec_master.shape[0]
    every = lax.all_gather(vec_master, ("dp", "tensor"), axis=0, tiled=True)
    halves = every.reshape(-1, 2, shard).transpose(1, 0, 2).reshape(2, 12, half)
    own = lax.dynamic_index_in_dim(halves, own_index, 0, keepdims=False)
    shared = jnp.concatenate([halves[0, 6:], halves[1, 6:]], axis=1)
    bias_query = own[0]
    bias_value = own[1]
    bias_up = own[2:6].reshape(-1)
    bias_out = shared[0]
    bias_down = shared[1]
    gain_one = shared[2]
    shift_one = shared[3]
    gain_two = shared[4]
    shift_two = shared[5]
    pairs = pair_index(pair_lengths, seq_len)
    valid = (pairs < pair_count).astype(jnp.float32).reshape(-1)
    x_float = tokens.astype(jnp.float32)
    projected = jnp.dot(tokens, w_project, preferred_element_type=jnp.float32)
    queries = (projected[:, :half] + bias_query).astype(jnp.bfloat16)
    keys = projected[:, half : 2 * half].astype(jnp.bfloat16)
    values = (projected[:, 2 * half :] + bias_value).astype(jnp.bfloat16)
    shape_four = (row_count, seq_len, heads_local, HD)
    query_rows = queries.reshape(shape_four)
    key_rows = keys.reshape(shape_four)
    value_rows = values.reshape(shape_four)
    contexts, tops, totals = lax.map(
        partial(row_forward, pair_count=pair_count, scale=scale, width=block_width),
        (query_rows, key_rows, value_rows, pairs),
    )
    context = contexts.reshape(-1, half)
    attention = (
        lax.psum(
            jnp.dot(context, w_out, preferred_element_type=jnp.float32).astype(jnp.bfloat16),
            "tensor",
        ).astype(jnp.float32)
        + bias_out
    )
    residual_one = x_float + attention
    hidden, normal_one, spread_one = layer_norm(residual_one, gain_one, shift_one)
    hidden_low = hidden.astype(jnp.bfloat16)
    pre_act = jnp.dot(hidden_low, w_up, preferred_element_type=jnp.float32) + bias_up
    act_low = jax.nn.gelu(pre_act, approximate=False).astype(jnp.bfloat16)
    feed = (
        lax.psum(
            jnp.dot(act_low, w_down, preferred_element_type=jnp.float32).astype(jnp.bfloat16),
            "tensor",
        ).astype(jnp.float32)
        + bias_down
    )
    residual_two = hidden + feed
    output, normal_two, spread_two = layer_norm(residual_two, gain_two, shift_two)
    mask = valid[:, None]
    squares = jnp.stack(
        [
            jnp.sum(mask * residual_one * residual_one),
            jnp.sum(mask * attention * attention),
            jnp.sum(mask * feed * feed),
        ]
    )
    squares, count = lax.psum((squares, jnp.sum(valid)), "dp")
    stream_rms = jnp.sqrt(squares / (count * width))
    grad_output = cotangent.astype(jnp.float32) * mask
    grad_two, grad_gain_two, grad_shift_two = norm_back(
        grad_output, normal_two, spread_two, gain_two
    )
    grad_bias_down = jnp.sum(grad_two, axis=0)
    grad_feed_low = grad_two.astype(jnp.bfloat16)
    grad_down = jnp.dot(act_low.T, grad_feed_low, preferred_element_type=jnp.float32)
    grad_act = jnp.dot(grad_feed_low, w_down.T, preferred_element_type=jnp.float32)
    grad_pre = grad_act * gelu_slope(pre_act)
    grad_bias_up = jnp.sum(grad_pre, axis=0)
    grad_pre_low = grad_pre.astype(jnp.bfloat16)
    grad_up = jnp.dot(hidden_low.T, grad_pre_low, preferred_element_type=jnp.float32)
    feed_blocks = jnp.stack([to_blocks(grad_up, edge), to_blocks(grad_down, edge)])
    grad_hidden = grad_two + lax.psum(
        jnp.dot(grad_pre_low, w_up.T, preferred_element_type=jnp.float32).astype(jnp.bfloat16),
        "tensor",
    ).astype(jnp.float32)
    grad_one, grad_gain_one, grad_shift_one = norm_back(
        grad_hidden, normal_one, spread_one, gain_one
    )
    grad_bias_out = jnp.sum(grad_one, axis=0)
    grad_attention_low = grad_one.astype(jnp.bfloat16)
    grad_out_weight = jnp.dot(context.T, grad_attention_low, preferred_element_type=jnp.float32)
    grad_context = jnp.dot(grad_attention_low, w_out.T, preferred_element_type=jnp.float32).astype(
        jnp.bfloat16
    )
    grad_queries, grad_keys, grad_values = lax.map(
        partial(row_backward, pair_count=pair_count, scale=scale, width=block_width),
        (query_rows, key_rows, value_rows, grad_context.reshape(shape_four), pairs, tops, totals),
    )
    grad_queries = grad_queries.reshape(-1, half)
    grad_keys = grad_keys.reshape(-1, half)
    grad_values = grad_values.reshape(-1, half)
    grad_bias_query = jnp.sum(grad_queries, axis=0)
    grad_bias_value = jnp.sum(grad_values, axis=0)
    grad_project_low = jnp.concatenate([grad_queries, grad_keys, grad_values], axis=1).astype(
        jnp.bfloat16
    )
    grad_project = jnp.dot(tokens.T, grad_project_low, preferred_element_type=jnp.float32)
    input_grad = grad_one + lax.psum(
        jnp.dot(grad_project_low, w_project.T, preferred_element_type=jnp.float32).astype(
            jnp.bfloat16
        ),
        "tensor",
    ).astype(jnp.float32)
    project_blocks = (
        grad_project.reshape(grid_model, edge, 3, grid_half, edge)
        .transpose(2, 0, 3, 1, 4)
        .reshape(3 * quarter, edge, edge)
    )
    attention_blocks = jnp.concatenate([project_blocks, to_blocks(grad_out_weight, edge)], axis=0)

    def own_half(vector):
        return lax.dynamic_slice_in_dim(vector, own_index * half, half)

    vec_local = jnp.concatenate(
        [
            grad_bias_query,
            grad_bias_value,
            grad_bias_up,
            own_half(grad_bias_out),
            own_half(grad_bias_down),
            own_half(grad_gain_one),
            own_half(grad_shift_one),
            own_half(grad_gain_two),
            own_half(grad_shift_two),
        ]
    )
    owned, vec_grads = (
        lax.psum_scatter(
            jnp.concatenate([attention_blocks[None], feed_blocks], axis=0),
            "dp",
            scatter_dimension=1,
            tiled=True,
        ),
        lax.psum_scatter(vec_local, "dp", scatter_dimension=0, tiled=True),
    )
    mat_grads = owned.reshape(-1, edge, edge)
    left_new = DECAY * mat_left + (1.0 - DECAY) * jnp.einsum(
        "bij,bkj->bik", mat_grads, mat_grads, precision=HIGHEST
    )
    right_new = DECAY * mat_right + (1.0 - DECAY) * jnp.einsum(
        "bji,bjk->bik", mat_grads, mat_grads, precision=HIGHEST
    )
    turned = jnp.einsum("bij,bjk->bik", root_left, mat_grads, precision=HIGHEST)
    turned = jnp.einsum("bij,bjk->bik", turned, root_right, precision=HIGHEST)
    mat_new = mat_master - STEP_RATE * turned
    second_new = DECAY * vec_second + (1.0 - DECAY) * vec_grads * vec_grads
    vec_new = vec_master - VEC_RATE * vec_grads / (jnp.sqrt(second_new) + VEC_EPS)
    return (
        output.astype(jnp.bfloat16),
        input_grad,
        mat_grads,
        left_new,
        right_new,
        mat_new,
        vec_grads,
        second_new,
        vec_new,
        stream_rms,
    )


def solution(mesh):
    placed = (
        P("dp", None),
        P("dp", None),
        P("dp", None),
        P(("dp", "tensor"), None, None),
        P(("dp", "tensor"), None, None),
        P(("dp", "tensor"), None, None),
        P(("dp", "tensor"), None, None),
        P(("dp", "tensor"), None, None),
        P(("dp", "tensor")),
        P(("dp", "tensor")),
    )
    return jax.shard_map(
        body,
        mesh=mesh,
        in_specs=placed,
        out_specs=(
            P("dp", None),
            P("dp", None),
            P(("dp", "tensor"), None, None),
            P(("dp", "tensor"), None, None),
            P(("dp", "tensor"), None, None),
            P(("dp", "tensor"), None, None),
            P(("dp", "tensor")),
            P(("dp", "tensor")),
            P(("dp", "tensor")),
            P(),
        ),
        check_vma=False,
    )
```

profile of v0, /device:TPU:0, one launch (start us, length us, event | category | flops | bytes accessed | tf_op | source)
XLA Modules:
  0.0 958.8 jit_solution(17430867888984673150)
XLA Ops:
  11.3 42.8 %all-reduce = f32[9216]{0:T(1024)S(1)} all-reduce(f32[9216]{0:T(1024)S(1)} %dynamic-update-slice), channel_id=1, replica_groups=mesh['dp'=16,'tensor'=2] {'dp','tensor'}, use_global_device_ids=true, to_apply=%add | all-reduce | flops 9216 | bytes 73728
  54.5 83.2 %all-gather.2.cloned.1.call-done = bf16[3,128,96,96]{3,2,1,0:T(8,128)(2,1)} async-done(((bf16[3,8,96,96]{3,2,1,0:T(8,128)(2,1)}), bf16[3,128,96,96]{3,2,1,0:T(8,128)(2,1)}) %all-gather.2.cloned.1.call-update) | async-done | bytes 7077904 | tf_op jit(solution)/shard_map/all_gather | solution.py:176
  150.0 6.8 fusion.121
  185.4 66.0 %while.28 = (s32[]{:T(128)}, bf16[2,1024,6,64]{1,3,2,0:T(8,128)(2,1)}, f32[2,2,6,512,1]{3,2,1,4,0:T(8,128)}, f32[2,2,6,512,1]{3,2,1,4,0:T(8,128)}, bf16[2,1024,6...) while((s32[]{:T(128)}, ...), condition=%wide.region_7.8_spmd, body=%wide.region_2.7_spmd.sunk | while | flops 1702763520 | bytes 105214704 | solution.py:216
  189.9 4.4 fusion.187
  261.5 5.6 fusion.117
  270.1 5.0 reshape.407
  275.1 5.0 copy.126
  280.1 6.5 reshape.406
  293.8 33.9 %fusion.71 = (bf16[2048,1536]{1,0:T(8,128)(2,1)S(1)}, f32[2048,1536]{1,0:T(8,128)}) fusion(f32[1536]{0:T(1024)S(1)} %copy-done.65, bf16[768,1536]{1,0:T(8,128)(2,1)S(1)} %copy-done.23, f32[768]{0:T(1024)S(1)} %copy-done.56, f32[768]{0:T(1024)S(1)} %copy-done.51, f32[2048]{0:T(1024)S(1)} %add_rsqrt_fusion.1, f32[2048]{0:T(1024)S(1)} %broadcast_multiply_fusion.5, ...), kind=kOutput, calls=%fused_computation.115 | convolution fusion | flops 5053612032 | bytes 27556864 | tf_op jit(solution)/shard_map/dot_general | solution.py:231
  330.3 6.3 convolution_convert_fusion.3
  337.3 21.1 %all-reduce.10.cloned.1.call-done = bf16[2048,768]{1,0:T(8,128)(2,1)} async-done(((bf16[2048,768]{1,0:T(8,128)(2,1)}), bf16[2048,768]{1,0:T(8,128)(2,1)}) %all-reduce.10.cloned.1.call-update) | async-done | bytes 3145744 | tf_op jit(solution)/shard_map/psum | solution.py:234
  358.4 5.6 fusion.115
  374.0 13.7 %fusion.120 = (f32[1536]{0:T(1024)}, bf16[2048,1536]{1,0:T(8,128)(2,1)S(1)}) fusion(f32[2048,1536]{1,0:T(8,128)} %get-tuple-element.329, f32[1536]{0:T(1024)S(1)} %copy-done.66, bf16[1536,768]{1,0:T(8,128)(2,1)S(1)} %reshape.407, f32[2048,768]{1,0:T(8,128)S(1)} %get-tuple-element.318), kind=kOutput, calls=%fused_computation.242 | convolution fusion | flops 4871158272 | bytes 27537408 | tf_op jit(solution)/shard_map/dot_general | solution.py:259
  390.4 6.4 convolution_convert_fusion.2
  396.9 24.5 %all-reduce.12.cloned.1.call-done = bf16[2048,768]{1,0:T(8,128)(2,1)} async-done(((bf16[2048,768]{1,0:T(8,128)(2,1)}), bf16[2048,768]{1,0:T(8,128)(2,1)}) %all-reduce.12.cloned.1.call-update) | async-done | bytes 3145744 | tf_op jit(solution)/shard_map/psum | solution.py:265
  421.4 12.9 %multiply_reduce_fusion.3 = (f32[768]{0:T(1024)}, f32[2048]{0:T(1024)S(1)}, f32[2048]{0:T(1024)S(1)}, f32[768]{0:T(1024)}, f32[]{:T(128)}, /*index=5*/f32[768]{0:T(1024)}, f32[]{:T(128)}, f32[]{:T(128)}) fusion(f32[2048,768]{1,0:T(8,128)} %copy-done.12, bf16[2048,768]{1,0:T(8,128)(2,1)} %all-reduce.12.cloned.1.call-done, f32[2048]{0:T(1024)S(1)} %copy-done.47, ...), kind=kLoop, calls=%fused_computation.144 | loop fusion | flops 42460928 | bytes 18933772 | tf_op jit(solution)/shard_map/reduce_sum | solution.py:62
  434.3 6.1 fusion.114
  455.8 123.3 %while.29 = (s32[]{:T(128)}, f32[2,1024,6,64]{1,3,2,0:T(8,128)}, bf16[2,1024,6,64]{1,3,2,0:T(8,128)(2,1)}, f32[2,1024,6,64]{1,3,2,0:T(8,128)}, bf16[2,1024,6,64]...) while((s32[]{:T(128)}, f32[2,1024,6,64]{1,3,2,0:T(8,128)}, ...), condition=%wide.region_22.23_spmd, body=%wide.region_19.22_spmd.sunk | while | flops 4099795968 | bytes 294897600 | solution.py:278
  460.0 9.2 multiply_reduce_fusion.11
  469.2 5.6 multiply_convert_fusion.4
  474.8 5.8 fusion.212
  484.5 9.2 multiply_reduce_fusion.12
  493.7 8.3 multiply_convert_fusion.5
  502.0 7.2 bitcast_dynamic-update-slice_fusion.5
  521.3 9.2 multiply_reduce_fusion.11
  530.5 5.6 multiply_convert_fusion.4
  536.1 5.8 fusion.212
  545.8 9.2 multiply_reduce_fusion.12
  555.0 8.3 multiply_convert_fusion.5
  563.3 7.2 bitcast_dynamic-update-slice_fusion.5
  579.1 5.4 fusion.118
  593.5 5.8 convolution_convert_fusion
  599.4 12.5 %fusion.96 = f32[768,1536]{1,0:T(8,128)} fusion(bf16[2048,1536]{1,0:T(8,128)(2,1)} %copy-done.72, f32[768]{0:T(1024)S(1)} %copy-done.57, f32[768]{0:T(1024)S(1)} %copy-done.53, bf16[2048,768]{1,0:T(8,128)(2,1)} %all-reduce.8.cloned.1.call-done, bf16[2048,768]{1,0:T(8,128)(2,1)} %param.14, f32[2048]{0:T(1024)S(1)} %copy-done.48, f32[2048]{0:T(1024)S(1)} %copy-done.39, ...), kind=kOutput, calls=%fused_computation.178 | convolution fusion | flops 4845993984 | bytes 17327104 | tf_op jit(solution)/shard_map/dot_general | solution.py:263
  611.9 7.6 reshape.415
  619.5 8.1 copy.140
  627.7 8.6 fusion.100
  636.3 7.7 reshape.416
  644.0 6.7 copy.141
  650.7 5.7 convolution_bitcast_fusion
  656.4 5.6 reshape.412
  662.1 6.3 copy.138
  668.4 10.1 %convert_bitcast_fusion = (bf16[768,2048]{0,1:T(8,128)(2,1)}, f32[2048,768]{1,0:T(8,128)}) fusion(f32[2048,768]{1,0:T(8,128)} %copy-done.13, bf16[2048,768]{1,0:T(8,128)(2,1)} %all-reduce.14.cloned.1.call-done), kind=kLoop, calls=%fused_computation.182 | loop fusion | flops 4718592 | bytes 18874368 | tf_op jit(solution)/shard_map/dot_general | solution.py:274
  678.5 4.7 copy.139
  691.3 7.0 copy_bitcast_fusion
  698.3 17.0 %reshape.423 = f32[128,27648]{1,0:T(8,128)} reshape(f32[128,3,96,96]{3,2,1,0:T(8,128)} %copy_bitcast_fusion) | data formatting | bytes 28311552
  720.6 79.9 %all-reduce.2 = (f32[4608]{0:T(1024)S(1)}, f32[3]{0:T(128)S(1)}, f32[]{:T(128)}) all-reduce(f32[4608]{0:T(1024)S(1)} %constant_dynamic-update-slice_fusion.6, f32[3]{0:T(128)S(1)} %pad_maximum_fusion.2, f32[]{:T(128)} %fusion.108), channel_id=3, replica_groups=mesh['dp'=16,'tensor'=2] {'dp'}, use_global_device_ids=true, to_apply=%region_34.35.clone | all-reduce | flops 4612 | bytes 36896
  802.4 137.0 %reduce-scatter.4.cloned.1.call-done = f32[8,27648]{1,0:T(8,128)} async-done(((f32[128,27648]{1,0:T(8,128)}), f32[8,27648]{1,0:T(8,128)}) %reduce-scatter.4.cloned.1.call-update) | async-done | bytes 884752
  (342 shorter events, 212.7 us)
Async XLA Ops:
  7.2 933.9 %copy-start = (f32[24,96,96]{2,1,0:T(8,128)S(1)}, f32[24,96,96]{2,1,0:T(8,128)}, u32[]{:S(2)}) copy-start(f32[24,96,96]{2,1,0:T(8,128)} %param.20) | copy-start | bytes 2654212
  7.2 130.5 %all-gather.2.cloned.1.call-start = ((), (), s32[]{:S(2)}) async-start(), calls=%async_computation.1 | async-start | bytes 10027008 | tf_op jit(solution)/shard_map/all_gather | solution.py:176
  9.5 277.1 %all-reduce.8.cloned.1.call-start = ((), (), s32[]{:S(2)}) async-start(), calls=%async_computation.2 | async-start | bytes 6291456 | tf_op jit(solution)/shard_map/psum | solution.py:222
  54.4 84.5 %copy-start.44 = (f32[2,12,384]{2,1,0:T(8,128)}, f32[2,12,384]{2,1,0:T(8,128)S(1)}, u32[]{:S(2)}) copy-start(f32[2,12,384]{2,1,0:T(8,128)S(1)} %reshape.400) | copy-start | bytes 110596
  251.4 8.7 copy-start.2
  260.2 98.2 %all-reduce.10.cloned.1.call-start = ((), (), s32[]{:S(2)}) async-start(), calls=%async_computation.3 | async-start | bytes 6291456 | tf_op jit(solution)/shard_map/psum | solution.py:234
  261.5 25.1 %copy-start.40 = (f32[768]{0:T(1024)}, f32[768]{0:T(1024)S(1)}, u32[]{:S(2)}) copy-start(f32[768]{0:T(1024)S(1)} %get-tuple-element.231) | copy-start | bytes 9220
  286.6 7.1 copy-start.23
  286.6 7.1 copy-start.51
  286.6 7.1 copy-start.56
  286.6 7.1 copy-start.65
  291.3 143.0 %copy-start.38 = (f32[2048]{0:T(1024)}, f32[2048]{0:T(1024)S(1)}, u32[]{:S(2)}) copy-start(f32[2048]{0:T(1024)S(1)} %broadcast_multiply_fusion.5) | copy-start | bytes 24580
  293.7 34.0 %copy-start.46 = (f32[2048]{0:T(1024)}, f32[2048]{0:T(1024)S(1)}, u32[]{:S(2)}) copy-start(f32[2048]{0:T(1024)S(1)} %add_rsqrt_fusion.1) | copy-start | bytes 24580
  336.6 84.7 %all-reduce.12.cloned.1.call-start = ((), (), s32[]{:S(2)}) async-start(), calls=%async_computation.4 | async-start | bytes 6291456 | tf_op jit(solution)/shard_map/psum | solution.py:265
  374.0 13.7 %copy-start.12 = (f32[2048,768]{1,0:T(8,128)}, f32[2048,768]{1,0:T(8,128)S(1)}, u32[]{:S(2)}) copy-start(f32[2048,768]{1,0:T(8,128)S(1)} %get-tuple-element.318) | copy-start | bytes 18874372
  374.0 16.3 %copy-start.24 = (bf16[768,1536]{1,0:T(8,128)(2,1)S(1)}, bf16[768,1536]{1,0:T(8,128)(2,1)}, u32[]{:S(2)}) copy-start(bf16[768,1536]{1,0:T(8,128)(2,1)} %reshape.406) | copy-start | bytes 7077892
  390.3 31.0 %copy-start.42 = (f32[768]{0:T(1024)S(1)}, f32[768]{0:T(1024)}, u32[]{:S(2)}) copy-start(f32[768]{0:T(1024)} %copy-done.40) | copy-start | bytes 9220
  390.3 31.0 %copy-start.47 = (f32[2048]{0:T(1024)S(1)}, f32[2048]{0:T(1024)}, u32[]{:S(2)}) copy-start(f32[2048]{0:T(1024)} %copy-done.46) | copy-start | bytes 24580
  390.3 31.0 %copy-start.50 = (f32[1,8,2,128]{3,1,2,0:T(8,128)S(1)}, f32[1,8,2,128]{3,1,2,0:T(8,128)}, u32[]{:S(2)}) copy-start(f32[1,8,2,128]{3,1,2,0:T(8,128)} %copy.158) | copy-start | bytes 24580
  390.3 31.0 %copy-start.52 = (f32[768]{0:T(1024)S(1)}, f32[768]{0:T(1024)}, u32[]{:S(2)}) copy-start(f32[768]{0:T(1024)} %get-tuple-element.230) | copy-start | bytes 9220
  390.4 31.0 %copy-start.54 = (f32[768]{0:T(1024)S(1)}, f32[768]{0:T(1024)}, u32[]{:S(2)}) copy-start(f32[768]{0:T(1024)} %get-tuple-element.228) | copy-start | bytes 9220
  396.8 271.6 %all-reduce.14.cloned.1.call-start = ((), (), s32[]{:S(2)}) async-start(), calls=%async_computation.5 | async-start | bytes 6291456 | tf_op jit(solution)/shard_map/psum | solution.py:291
  421.4 12.9 %copy-start.5 = (bf16[2048,768]{1,0:T(8,128)(2,1)S(1)}, bf16[2048,768]{1,0:T(8,128)(2,1)}, u32[]{:S(2)}) copy-start(bf16[2048,768]{1,0:T(8,128)(2,1)} %param.14) | copy-start | bytes 9437188
  421.4 12.9 %copy-start.8 = (bf16[2048,768]{1,0:T(8,128)(2,1)S(1)}, bf16[2048,768]{1,0:T(8,128)(2,1)}, u32[]{:S(2)}) copy-start(bf16[2048,768]{1,0:T(8,128)(2,1)} %all-reduce.8.cloned.1.call-done) | copy-start | bytes 9437188
  421.4 12.9 %copy-start.17 = (bf16[2048,768]{1,0:T(8,128)(2,1)S(1)}, bf16[2048,768]{1,0:T(8,128)(2,1)}, u32[]{:S(2)}) copy-start(bf16[2048,768]{1,0:T(8,128)(2,1)} %all-reduce.12.cloned.1.call-done) | copy-start | bytes 9437188
  434.3 8.8 copy-start.22
  446.1 9.7 %copy-start.3 = (bf16[2,1024,6,64]{1,3,2,0:T(8,128)(2,1)S(1)}, bf16[2,1024,6,64]{1,3,2,0:T(8,128)(2,1)}, u32[]{:S(2)}) copy-start(bf16[2,1024,6,64]{1,3,2,0:T(8,128)(2,1)} %copy-done.2) | copy-start | bytes 4718596
  446.1 9.7 %copy-start.36 = (f32[2,2,6,512,1]{3,2,1,4,0:T(8,128)S(1)}, f32[2,2,6,512,1]{3,2,1,4,0:T(8,128)}, u32[]{:S(2)}) copy-start(f32[2,2,6,512,1]{3,2,1,4,0:T(8,128)} %get-tuple-element.211) | copy-start | bytes 147460
  446.1 9.7 %copy-start.37 = (f32[2,2,6,512,1]{3,2,1,4,0:T(8,128)S(1)}, f32[2,2,6,512,1]{3,2,1,4,0:T(8,128)}, u32[]{:S(2)}) copy-start(f32[2,2,6,512,1]{3,2,1,4,0:T(8,128)} %get-tuple-element.210) | copy-start | bytes 147460
  502.0 7.2 copy-start.1
  563.3 7.2 copy-start.1
  593.5 5.9 copy-start.48
  593.5 5.9 copy-start.53
  593.5 5.9 copy-start.57
  599.3 340.1 %reduce-scatter.4.cloned.1.call-start = ((), (), s32[]{:S(2)}) async-start(), calls=%async_computation.6 | async-start | bytes 15040512
  611.9 15.8 %slice-start = ((s8[6291456]{0:T(1024)(128)(4,1)}), s8[2097152]{0:T(1024)(128)(4,1)S(1)}, s32[]{:S(2)}) async-start(s8[6291456]{0:T(1024)(128)(4,1)} %bitcast.340), calls=%async_computation.7 | async-start | bytes 4194304
  619.5 8.1 slice-start.1
  636.3 14.4 %slice-start.6 = ((s8[4718592]{0:T(1024)(128)(4,1)}), s8[524288]{0:T(1024)(128)(4,1)S(1)}, s32[]{:S(2)}) async-start(s8[4718592]{0:T(1024)(128)(4,1)} %bitcast.372), calls=%async_computation.13 | async-start | bytes 1048576
  644.0 6.7 copy-start.6
  644.0 6.7 slice-start.7
  683.2 7.5 slice-start.2
  683.2 7.5 slice-start.4
  715.4 86.3 %copy-start.67 = (f32[288]{0:T(512)S(1)}, f32[288]{0:T(512)}, u32[]{:S(2)}) copy-start(f32[288]{0:T(512)} %param.22) | copy-start | bytes 3460
  715.4 86.3 %copy-start.69 = (f32[288]{0:T(512)S(1)}, f32[288]{0:T(512)}, u32[]{:S(2)}) copy-start(f32[288]{0:T(512)} %param.23) | copy-start | bytes 3460
  715.5 226.9 %copy-start.32 = (f32[24,96,96]{2,1,0:T(8,128)S(1)}, f32[24,96,96]{2,1,0:T(8,128)}, u32[]{:S(2)}) copy-start(f32[24,96,96]{2,1,0:T(8,128)} %param.19) | copy-start | bytes 2654212
  941.1 8.1 copy-start.15
  941.1 8.0 copy-start.18
  941.1 8.0 copy-start.34
  (50 other events, 165.8 us)
Sparse Core Ops, SparseCore 0:
  11.3 126.3 all-gather.1
  260.3 21.3 all-reduce.7
  336.8 21.5 all-reduce.9
  396.9 24.3 all-reduce.11
  599.4 24.3 all-reduce.13
  715.6 223.7 reduce-scatter.3
where the time goes:
time: 970 us; the launch traced here: 959 us
  waiting for transfers between devices  266 us (27%)
  matrix products  237 us (24%)
  local copies, waits for them, and re-layouts  177 us (18%)
  other arithmetic  126 us (13%)
  blocking collectives  123 us (13%)
  between operations  16.8 us (2%)
  loops' own time  12.9 us (1%)
    unnamed x7, waiting for transfers between devices  137 us
    unnamed x2, blocking collectives  123 us
    all_gather x1, waiting for transfers between devices, body(): blocks = lax.all_gather(local_blocks, 'dp', axis=1, tiled=True)  83.2 us
    dot_general x8, matrix products, block_scores(): jnp.einsum('qhd,khd->hqk', query_blk, key_row, preferred_element_type=jnp...  50.3 us
    unnamed x161, local copies, waits for them, and re-layouts  37.3 us
    dot_general x1, matrix products, body(): jnp.dot(hidden_low, w_up, preferred_element_type=jnp.float32) + bias_up  33.9 us
    reshape x4, local copies, waits for them, and re-layouts, to_blocks(): matrix.reshape(grid_rows, edge, grid_cols, edge).transpose(0, 2, 1, 3)  30.1 us
    convert_element_type x4, other arithmetic, block_backward(): grad_scores = (probs * (grad_probs - centre)).astype(jnp.bfloat16)  27.8 us
  transfers between devices with their start and end apart: 6, of which 4 were waited for; matrix products, arithmetic and copies ran while one was open for 11% of the time, Pallas kernels for 0%

commit v1 on v0

v1 whole, which is shorter than its diff:
```python
from functools import partial
import math

import jax
import jax.numpy as jnp
from jax import lax
from jax.experimental import pallas as pl
from jax.experimental.pallas import tpu as pltpu
from jax.sharding import PartitionSpec as P

HD = 64
LN_EPS = 1e-12
BIG = 1e30
FLOOR = -1e29
DECAY = 0.5
STEP_RATE = 1.0
VEC_RATE = 0.1
VEC_EPS = 1e-08
INV_ROOT_TWO = 1.0 / math.sqrt(2.0)
INV_ROOT_TWO_PI = 1.0 / math.sqrt(2.0 * math.pi)
BF = jnp.bfloat16
F32 = jnp.float32
LANES = 128
VMEM_LIMIT = 60 * 2**20
MESH = pl.DeviceIdType.MESH


def nn(a, b):
    return lax.dot_general(a, b, (((1,), (0,)), ((), ())), preferred_element_type=F32)


def nt(a, b):
    return lax.dot_general(a, b, (((1,), (1,)), ((), ())), preferred_element_type=F32)


def tn(a, b):
    return lax.dot_general(a, b, (((0,), (0,)), ((), ())), preferred_element_type=F32)


def unblock(blocks, grid_rows, grid_cols):
    edge = blocks.shape[-1]
    return (
        blocks.reshape(grid_rows, grid_cols, edge, edge)
        .transpose(0, 2, 1, 3)
        .reshape(grid_rows * edge, grid_cols * edge)
    )


def to_blocks(matrix, edge):
    grid_rows = matrix.shape[0] // edge
    grid_cols = matrix.shape[1] // edge
    return (
        matrix.reshape(grid_rows, edge, grid_cols, edge)
        .transpose(0, 2, 1, 3)
        .reshape(grid_rows * grid_cols, edge, edge)
    )


def erf_parts(u):
    z = jnp.abs(u) * INV_ROOT_TWO
    gauss = jnp.exp(-z * z)
    t = 1.0 / (1.0 + 0.3275911 * z)
    poly = t * (
        0.254829592
        + t * (-0.284496736 + t * (1.421413741 + t * (-1.453152027 + t * 1.061405429)))
    )
    tail = poly * gauss
    return jnp.where(u >= 0.0, 2.0 - tail, tail), gauss


def params(**kw):
    return pltpu.CompilerParams(vmem_limit_bytes=VMEM_LIMIT, **kw)


def low_lanes(shape):
    return lax.broadcasted_iota(jnp.int32, shape, 1) < HD


def attn_fwd_kernel(
    tok, w_qkv, w_out, bias, hot, cold, qkv, ctx, lse, part, *, half, seq, blk
):
    heads = half // HD
    qkv[...] = (nn(tok[...], w_qkv[...]) + bias[...]).astype(BF)
    low = low_lanes((blk, LANES))
    lane = lax.broadcasted_iota(jnp.int32, (blk, LANES), 1)

    def step(index, carry):
        rows = pl.ds(pl.multiple_of(index * blk, blk), blk)
        hot_blk = hot[0, rows, :]
        stats = jnp.zeros((blk, LANES), F32)
        for pair in range(heads // 2):
            cols = pl.ds(pair * LANES, LANES)
            q_pair = qkv[rows, cols] * jnp.asarray(HD**-0.5, BF)
            k_aug = jnp.concatenate(
                [qkv[:, pl.ds(half + pair * LANES, LANES)], cold[0]], axis=1
            )
            v_pair = qkv[:, pl.ds(2 * half + pair * LANES, LANES)]
            outs = []
            for side in range(2):
                own = low if side == 0 else jnp.logical_not(low)
                q_aug = jnp.concatenate([jnp.where(own, q_pair, 0), hot_blk], axis=1)
                s = nt(q_aug, k_aug)
                top = jnp.maximum(jnp.max(s, axis=1, keepdims=True), FLOOR)
                e = jnp.exp(s - top)
                total = jnp.maximum(jnp.sum(e, axis=1, keepdims=True), 0.5)
                outs.append(nn(e.astype(BF), v_pair) / total)
                stats = jnp.where(lane == 2 * pair + side, top + jnp.log(total), stats)
            ctx[rows, cols] = jnp.where(low, outs[0], outs[1]).astype(BF)
        lse[0, :, rows] = stats.T[: lse.shape[1]]
        return carry

    lax.fori_loop(0, seq // blk, step, 0)
    part[...] = nn(ctx[...], w_out[...]).astype(BF)


def attn_fwd(tok, w_qkv, w_out, bias, hot, cold, rows, seq):
    width = tok.shape[1]
    half = width // 2
    stat_rows = -(-(half // HD) // 8) * 8
    whole = lambda shape: pl.BlockSpec(shape, lambda r: (0,) * len(shape))
    return pl.pallas_call(
        partial(attn_fwd_kernel, half=half, seq=seq, blk=256),
        grid=(rows,),
        in_specs=[
            pl.BlockSpec((seq, width), lambda r: (r, 0)),
            whole((width, 3 * half)),
            whole((half, width)),
            whole((1, 3 * half)),
            pl.BlockSpec((1, seq, LANES), lambda r: (r, 0, 0)),
            pl.BlockSpec((1, seq, LANES), lambda r: (r, 0, 0)),
        ],
        out_specs=[
            pl.BlockSpec((seq, 3 * half), lambda r: (r, 0)),
            pl.BlockSpec((seq, half), lambda r: (r, 0)),
            pl.BlockSpec((1, stat_rows, seq), lambda r: (r, 0, 0)),
            pl.BlockSpec((seq, width), lambda r: (r, 0)),
        ],
        out_shape=[
            jax.ShapeDtypeStruct((rows * seq, 3 * half), BF),
            jax.ShapeDtypeStruct((rows * seq, half), BF),
            jax.ShapeDtypeStruct((rows, stat_rows, seq), F32),
            jax.ShapeDtypeStruct((rows * seq, width), BF),
        ],
        compiler_params=params(),
        name="attn_fwd",
    )(tok, w_qkv, w_out, bias, hot, cold)


def attn_bwd_kernel(
    gattn, qkv, ctx, lse, w_qkv, w_out, hot, cold, gqkv, sums, part, gctx, centre, dk, dv,
    *, half, seq, blk,
):
    heads = half // HD
    g = nt(gattn[...], w_out[...])
    gctx[...] = g.astype(BF)
    prod = gctx[...].astype(F32) * ctx[...].astype(F32)
    picks = (
        lax.broadcasted_iota(jnp.int32, (8, half), 0)
        == lax.broadcasted_iota(jnp.int32, (8, half), 1) // HD
    ).astype(F32)
    centre[...] = lax.dot_general(
        picks, prod, (((1,), (1,)), ((), ())),
        preferred_element_type=F32, precision=lax.Precision.HIGHEST,
    )
    low = low_lanes((blk, LANES))
    scale = jnp.asarray(HD**-0.5, BF)
    for pair in range(heads // 2):
        cols = pl.ds(pair * LANES, LANES)
        dk[...] = jnp.zeros_like(dk)
        dv[...] = jnp.zeros_like(dv)

        def step(index, gq_sum):
            rows = pl.ds(pl.multiple_of(index * blk, blk), blk)
            hot_blk = hot[0, rows, :]
            q_pair = qkv[rows, cols] * scale
            g_pair = gctx[rows, cols]
            k_pair = qkv[:, pl.ds(half + pair * LANES, LANES)]
            k_aug = jnp.concatenate([k_pair, cold[0]], axis=1)
            v_pair = qkv[:, pl.ds(2 * half + pair * LANES, LANES)]
            outs = []
            dk_new = dk[...]
            dv_new = dv[...]
            for side in range(2):
                head = 2 * pair + side
                own = low if side == 0 else jnp.logical_not(low)
                q_own = jnp.where(own, q_pair, 0)
                g_own = jnp.where(own, g_pair, 0)
                s = nt(k_aug, jnp.concatenate([q_own, hot_blk], axis=1))
                p = jnp.exp(s - lse[0, pl.ds(head, 1), rows])
                gp = nt(v_pair, g_own)
                gs = (p * (gp - centre[pl.ds(head, 1), rows])).astype(BF)
                dv_new = dv_new + nn(p.astype(BF), g_own)
                dk_new = dk_new + nn(gs, q_own)
                outs.append(tn(gs, k_pair))
            dk[...] = dk_new
            dv[...] = dv_new
            gq = jnp.where(low, outs[0], outs[1]) * HD**-0.5
            gqkv[rows, cols] = gq.astype(BF)
            return gq_sum + jnp.sum(gq, axis=0, keepdims=True)

        gq_sum = lax.fori_loop(0, seq // blk, step, jnp.zeros((1, LANES), F32))
        gqkv[:, pl.ds(half + pair * LANES, LANES)] = dk[...].astype(BF)
        gqkv[:, pl.ds(2 * half + pair * LANES, LANES)] = dv[...].astype(BF)
        sums[0, 0:1, cols] = gq_sum
        sums[0, 1:2, cols] = jnp.sum(dv[...], axis=0, keepdims=True)
    part[...] = nt(gqkv[...], w_qkv[...]).astype(BF)


def attn_bwd(gattn, qkv, ctx, lse, w_qkv, w_out, hot, cold, rows, seq):
    width = gattn.shape[1]
    half = width // 2
    whole = lambda shape: pl.BlockSpec(shape, lambda r: (0,) * len(shape))
    return pl.pallas_call(
        partial(attn_bwd_kernel, half=half, seq=seq, blk=256),
        grid=(rows,),
        in_specs=[
            pl.BlockSpec((seq, width), lambda r: (r, 0)),
            pl.BlockSpec((seq, 3 * half), lambda r: (r, 0)),
            pl.BlockSpec((seq, half), lambda r: (r, 0)),
            pl.BlockSpec((1, lse.shape[1], seq), lambda r: (r, 0, 0)),
            whole((width, 3 * half)),
            whole((half, width)),
            pl.BlockSpec((1, seq, LANES), lambda r: (r, 0, 0)),
            pl.BlockSpec((1, seq, LANES), lambda r: (r, 0, 0)),
        ],
        out_specs=[
            pl.BlockSpec((seq, 3 * half), lambda r: (r, 0)),
            pl.BlockSpec((1, 8, half), lambda r: (r, 0, 0)),
            pl.BlockSpec((seq, width), lambda r: (r, 0)),
        ],
        out_shape=[
            jax.ShapeDtypeStruct((rows * seq, 3 * half), BF),
            jax.ShapeDtypeStruct((rows, 8, half), F32),
            jax.ShapeDtypeStruct((rows * seq, width), BF),
        ],
        scratch_shapes=[
            pltpu.VMEM((seq, half), BF),
            pltpu.VMEM((8, seq), F32),
            pltpu.VMEM((seq, LANES), F32),
            pltpu.VMEM((seq, LANES), F32),
        ],
        compiler_params=params(),
        name="attn_bwd",
    )(gattn, qkv, ctx, lse, w_qkv, w_out, hot, cold)


def mean_last(x):
    return jnp.mean(x, axis=-1, keepdims=True)


def norm_back(grad, normal, inverse, gain):
    scaled = grad * gain
    return inverse * (scaled - mean_last(scaled) - normal * mean_last(scaled * normal))


def fold(x):
    return jnp.sum(x, axis=0, keepdims=True)


def feed_kernel(
    tok, cot, valid, part, part_all, w_up, w_down, b_up, vec,
    out, r1_grad, gattn, act, hid, gfeed, gpre, sums, up_sum,
    got1, send2, got2, send3, got3, normal1, inv1, grad2, slope, send_sem, recv_sem,
    *, tiles, blk,
):
    i = pl.program_id(0)
    other = 1 - lax.axis_index("tensor")
    width = tok.shape[1]
    hidden = w_up.shape[1]
    chunk = width

    def span(t):
        return pl.ds(pl.multiple_of(t * blk, blk), blk)

    def copy(stage, t):
        src = (part_all, send2, send3)[stage]
        dst = (got1, got2, got3)[stage]
        return pltpu.make_async_remote_copy(
            src_ref=src.at[span(t)],
            dst_ref=dst.at[span(t)],
            send_sem=send_sem.at[stage, t],
            recv_sem=recv_sem.at[stage, t],
            device_id={"tensor": other},
            device_id_type=MESH,
        )

    @pl.when(i == 0)
    def _():
        barrier = pltpu.get_barrier_semaphore()
        pl.semaphore_signal(barrier, inc=1, device_id={"tensor": other}, device_id_type=MESH)
        pl.semaphore_wait(barrier, 1)
        for t in range(tiles):
            copy(0, t).start()
        sums[...] = jnp.zeros_like(sums)
        up_sum[...] = jnp.zeros_like(up_sum)

    bias_out, bias_down = vec[0:1], vec[1:2]
    gain1, shift1, gain2, shift2 = vec[2:3], vec[3:4], vec[4:5], vec[5:6]

    @pl.when(i < tiles)
    def _():
        t = i
        slot = lax.rem(t, 3)
        copy(0, t).wait()
        keep = valid[0, :, :1]
        att = part[...].astype(F32) + got1[span(t)].astype(F32) + bias_out
        r1 = tok[...].astype(F32) + att
        centred = r1 - mean_last(r1)
        inverse = lax.rsqrt(mean_last(centred * centred) + LN_EPS)
        normal = centred * inverse
        normal1[slot] = normal
        inv1[slot] = jnp.broadcast_to(inverse, (blk, LANES))
        low = (normal * gain1 + shift1).astype(BF)
        hid[...] = low
        sums[6:7] += fold(keep * r1 * r1)
        sums[7:8] += fold(keep * att * att)
        for c in range(0, hidden, chunk):
            u = nn(low, w_up[:, c : c + chunk]) + b_up[:, c : c + chunk]
            both, gauss = erf_parts(u)
            act[:, c : c + chunk] = (0.5 * u * both).astype(BF)
            slope[lax.rem(t, 2), :, c : c + chunk] = (
                0.5 * both + u * gauss * INV_ROOT_TWO_PI
            ).astype(BF)
        send2[span(t)] = nn(act[...], w_down[...]).astype(BF)
        copy(1, t).start()

    @pl.when((i >= 1) & (i <= tiles))
    def _():
        t = i - 1
        copy(1, t).wait()
        keep = valid[1, :, :1]
        feed = send2[span(t)].astype(F32) + got2[span(t)].astype(F32) + bias_down
        r2 = normal1[lax.rem(t, 3)] * gain1 + shift1 + feed
        centred = r2 - mean_last(r2)
        inverse = lax.rsqrt(mean_last(centred * centred) + LN_EPS)
        normal = centred * inverse
        out[...] = (normal * gain2 + shift2).astype(BF)
        g = cot[...].astype(F32) * keep
        gr = norm_back(g, normal, inverse, gain2)
        grad2[lax.rem(t, 2)] = gr
        sums[1:2] += fold(gr)
        sums[4:5] += fold(g * normal)
        sums[5:6] += fold(g)
        sums[8:9] += fold(keep * feed * feed)
        low = gr.astype(BF)
        gfeed[...] = low
        for c in range(0, hidden, chunk):
            gu = nt(low, w_down[c : c + chunk]) * slope[lax.rem(t, 2), :, c : c + chunk].astype(F32)
            up_sum[0:1, c : c + chunk] += fold(gu)
            gpre[:, c : c + chunk] = gu.astype(BF)
        send3[span(t)] = nt(gpre[...], w_up[...]).astype(BF)
        copy(2, t).start()

    @pl.when(i >= 2)
    def _():
        t = i - 2
        slot = lax.rem(t, 3)
        copy(2, t).wait()
        gh = (
            grad2[lax.rem(t, 2)]
            + send3[span(t)].astype(F32)
            + got3[span(t)].astype(F32)
        )
        normal = normal1[slot]
        gr = norm_back(gh, normal, inv1[slot][:, :1], gain1)
        sums[0:1] += fold(gr)
        sums[2:3] += fold(gh * normal)
        sums[3:4] += fold(gh)
        r1_grad[...] = gr
        gattn[...] = gr.astype(BF)


def feed(tok, cot, valid, part, w_up, w_down, b_up, vec, blk=256):
    count, width = tok.shape
    hidden = w_up.shape[1]
    tiles = count // blk
    lag = lambda n: (lambda i: (jnp.clip(i - n, 0, tiles - 1), 0))
    whole = lambda shape: pl.BlockSpec(shape, lambda i: (0,) * len(shape))
    wide = lambda n: pl.BlockSpec((blk, width), lag(n))
    deep = lambda n: pl.BlockSpec((blk, hidden), lag(n))
    return pl.pallas_call(
        partial(feed_kernel_entry, tiles=tiles, blk=blk),
        grid=(tiles + 2,),
        in_specs=[
            wide(0),
            wide(1),
            pl.BlockSpec((blk, LANES), lag(0)),
            pl.BlockSpec((blk, LANES), lag(1)),
            wide(0),
            pl.BlockSpec(memory_space=pl.ANY),
            whole((width, hidden)),
            whole((hidden, width)),
            whole((1, hidden)),
            whole((8, width)),
        ],
        out_specs=[
            wide(1), wide(2), wide(2), deep(0), wide(0), wide(1), deep(1),
            whole((16, width)), whole((8, hidden)),
        ],
        out_shape=[
            jax.ShapeDtypeStruct((count, width), BF),
            jax.ShapeDtypeStruct((count, width), F32),
            jax.ShapeDtypeStruct((count, width), BF),
            jax.ShapeDtypeStruct((count, hidden), BF),
            jax.ShapeDtypeStruct((count, width), BF),
            jax.ShapeDtypeStruct((count, width), BF),
            jax.ShapeDtypeStruct((count, hidden), BF),
            jax.ShapeDtypeStruct((16, width), F32),
            jax.ShapeDtypeStruct((8, hidden), F32),
        ],
        scratch_shapes=[
            *[pltpu.VMEM((count, width), BF) for _ in range(5)],
            pltpu.VMEM((3, blk, width), F32),
            pltpu.VMEM((3, blk, LANES), F32),
            pltpu.VMEM((2, blk, width), F32),
            pltpu.VMEM((2, blk, hidden), BF),
            pltpu.SemaphoreType.DMA((3, tiles)),
            pltpu.SemaphoreType.DMA((3, tiles)),
        ],
        compiler_params=params(collective_id=1, has_side_effects=True),
        name="feed",
    )(tok, cot, valid, valid, part, part, w_up, w_down, b_up, vec)


class Both:
    def __init__(self, *refs):
        self.refs = refs

    def __getitem__(self, key):
        return self.refs[key[0]][key[1:]]


def feed_kernel_entry(tok, cot, valid0, valid1, *rest, tiles, blk):
    feed_kernel(tok, cot, Both(valid0, valid1), *rest, tiles=tiles, blk=blk)


def body(
    tokens,
    cotangent,
    pair_lengths,
    mat_master,
    mat_left,
    mat_right,
    root_left,
    root_right,
    vec_master,
    vec_second,
):
    width = tokens.shape[1]
    half = width // 2
    row_count, pair_count = pair_lengths.shape
    seq = tokens.shape[0] // row_count
    edge = mat_master.shape[-1]
    own_index = lax.axis_index("tensor")
    local = mat_master.astype(BF).reshape(3, -1, edge, edge)
    blocks = lax.all_gather(local, "dp", axis=1, tiled=True)
    kind_count = blocks.shape[1]
    quarter = kind_count // 4
    grid_model = width // edge
    grid_half = half // edge
    grid_hidden = kind_count // grid_model
    w_project = (
        blocks[0, : 3 * quarter]
        .reshape(3, grid_model, grid_half, edge, edge)
        .transpose(1, 3, 0, 2, 4)
        .reshape(width, 3 * half)
    )
    w_out = unblock(blocks[0, 3 * quarter :], grid_half, grid_model)
    w_up = unblock(blocks[1], grid_model, grid_hidden)
    w_down = unblock(blocks[2], grid_hidden, grid_model)
    shard = vec_master.shape[0]
    every = lax.all_gather(vec_master, ("dp", "tensor"), axis=0, tiled=True)
    halves = every.reshape(-1, 2, shard).transpose(1, 0, 2).reshape(2, 12, half)
    own = lax.dynamic_index_in_dim(halves, own_index, 0, keepdims=False)
    shared = jnp.concatenate([halves[0, 6:], halves[1, 6:]], axis=1)
    bias_up = own[2:6].reshape(1, -1)
    bias_qkv = jnp.concatenate([own[0], jnp.zeros((half,), F32), own[1]])[None]

    place = lax.broadcasted_iota(jnp.int32, (row_count, seq, pair_count), 1)
    upto = jnp.tril(jnp.ones((pair_count, pair_count), jnp.int32))
    ends = jnp.sum(pair_lengths[:, None, :] * upto[None], axis=-1)
    pairs = jnp.sum((place >= ends[:, None, :]).astype(jnp.int32), axis=-1)
    ids = lax.broadcasted_iota(jnp.int32, (row_count, seq, LANES), 2)
    same = pairs[:, :, None] == ids
    hot = same.astype(BF)
    cold = jnp.where(same & (ids < pair_count), 0.0, -BIG).astype(BF)
    keep = (pairs < pair_count).astype(F32).reshape(-1)
    valid = jnp.broadcast_to(keep[:, None], (keep.shape[0], LANES))

    qkv, ctx, lse, part = attn_fwd(tokens, w_project, w_out, bias_qkv, hot, cold, row_count, seq)
    vec_rows = jnp.concatenate([shared, jnp.zeros((2, width), F32)])
    block_out, gr1, gattn, act, hid, gfeed, gpre, sums, up_sum = feed(
        tokens, cotangent, valid, part, w_up, w_down, bias_up, vec_rows
    )
    grad_down = tn(act, gfeed).astype(BF)
    grad_up = tn(hid, gpre).astype(BF)
    gqkv, bias_sums, part_in = attn_bwd(
        gattn, qkv, ctx, lse, w_project, w_out, hot, cold, row_count, seq
    )
    grad_out_weight = tn(ctx, gattn).astype(BF)
    grad_project = tn(tokens, gqkv).astype(BF)
    swap = [(0, 1), (1, 0)]
    input_grad = gr1 + part_in.astype(F32) + lax.ppermute(part_in, "tensor", swap).astype(F32)

    squares, count = lax.psum((jnp.sum(sums[6:9], axis=1), jnp.sum(keep)), "dp")
    stream_rms = jnp.sqrt(squares / (count * width))

    project_blocks = (
        grad_project.reshape(grid_model, edge, 3, grid_half, edge)
        .transpose(2, 0, 3, 1, 4)
        .reshape(3 * quarter, edge, edge)
    )
    attention_blocks = jnp.concatenate([project_blocks, to_blocks(grad_out_weight, edge)], axis=0)
    feed_blocks = jnp.stack([to_blocks(grad_up, edge), to_blocks(grad_down, edge)])
    bias_pair = jnp.sum(bias_sums, axis=0)
    shared_sums = lax.dynamic_slice_in_dim(sums[:6], own_index * half, half, axis=1)
    vec_local = jnp.concatenate([bias_pair[:2].reshape(-1), up_sum[0], shared_sums.reshape(-1)])
    owned = lax.psum_scatter(
        jnp.concatenate([attention_blocks[None], feed_blocks], axis=0),
        "dp",
        scatter_dimension=1,
        tiled=True,
    )
    vec_grads = lax.psum_scatter(vec_local, "dp", scatter_dimension=0, tiled=True)
    mat_grads = owned.astype(F32).reshape(-1, edge, edge)
    left_new = DECAY * mat_left + (1.0 - DECAY) * jnp.einsum("bij,bkj->bik", mat_grads, mat_grads)
    right_new = DECAY * mat_right + (1.0 - DECAY) * jnp.einsum("bji,bjk->bik", mat_grads, mat_grads)
    turned = jnp.einsum("bij,bjk->bik", root_left, mat_grads)
    turned = jnp.einsum("bij,bjk->bik", turned, root_right)
    mat_new = mat_master - STEP_RATE * turned
    second_new = DECAY * vec_second + (1.0 - DECAY) * vec_grads * vec_grads
    vec_new = vec_master - VEC_RATE * vec_grads / (jnp.sqrt(second_new) + VEC_EPS)
    return (
        block_out,
        input_grad,
        mat_grads,
        left_new,
        right_new,
        mat_new,
        vec_grads,
        second_new,
        vec_new,
        stream_rms,
    )


def solution(mesh):
    blocks = P(("dp", "tensor"), None, None)
    rows = P("dp", None)
    entries = P(("dp", "tensor"))
    return jax.shard_map(
        body,
        mesh=mesh,
        in_specs=(rows, rows, rows, *[blocks] * 5, entries, entries),
        out_specs=(rows, rows, *[blocks] * 4, entries, entries, entries, P()),
        check_vma=False,
    )
```

time: 970 us -> 582 us (0.60)
  matrix products: 237 us -> 37.8 us
  Pallas kernels: 0 us -> 145 us
  waiting for transfers between devices: 266 us -> 140 us
  other arithmetic: 126 us -> 22.9 us
  local copies, waits for them, and re-layouts: 177 us -> 92 us
  loops' own time: 12.9 us -> 0 us
    dot_general x44 -> x7, matrix products: 237 us -> 37.8 us  [the longest x4 30.8 us: tn(): lax.dot_general(a, b, (((0,), (0,)), ((), ())), preferred_element_type=F32)]
    pallas_call x0 -> x3, Pallas kernels: none -> 145 us  [the longest x1 56.8 us: feed(): pl.pallas_call(partial(feed_kernel_entry, tiles=tiles, blk=blk), grid=(ti...]
    unnamed x7 -> x3, waiting for transfers between devices: 137 us -> 61.8 us
    reduce_sum x14 -> x5, other arithmetic: 60 us -> 1.66 us  [the longest x1 0.82 us: body(): ends = jnp.sum(pair_lengths[:, None, :] * upto[None], axis=-1)]
    psum x4 -> x0, waiting for transfers between devices: 45.6 us -> none  [the longest x1 24.5 us: body(): lax.psum(jnp.dot(grad_pre_low, w_up.T, preferred_element_type=jnp.float32...]
    convert_element_type x6 -> x3, other arithmetic: 32.2 us -> 4.52 us  [the longest x1 2.25 us: body(): local = mat_master.astype(BF).reshape(3, -1, edge, edge)]
    while x49 -> x0, local copies, waits for them, and re-layouts: 23.8 us -> none  [the longest x4 11.5 us: body(): lax.map(partial(row_forward, pair_count=pair_count, scale=scale, width=bl...]
    reshape x4 -> x2, local copies, waits for them, and re-layouts: 15.4 us -> 0.01 us  [the longest x1 0.01 us: body(): bias_pair[:2].reshape(-1)]
  transfers between devices with their start and end apart: 6 -> 3, of which waited for: 4 -> 2; matrix products, arithmetic and copies ran while one was open for 11% -> 3% of each run, Pallas kernels for 0% -> 0%
where the time goes in v1:
time: 582 us; the launch traced here: 573 us
  Pallas kernels  145 us (25%)
  waiting for transfers between devices  140 us (24%)
  blocking collectives  118 us (20%)
  local copies, waits for them, and re-layouts  92 us (16%)
  matrix products  37.8 us (6%)
  other arithmetic  22.9 us (4%)
  between operations  16.1 us (3%)
    unnamed x2, blocking collectives  118 us
    all_gather x1, waiting for transfers between devices, body(): blocks = lax.all_gather(local, 'dp', axis=1, tiled=True)  78.6 us
    unnamed x3, waiting for transfers between devices  61.8 us
    pallas_call x1, Pallas kernels, feed(): pl.pallas_call(partial(feed_kernel_entry, tiles=tiles, blk=blk), grid=(ti...  56.8 us
    pallas_call x1, Pallas kernels, attn_bwd(): pl.pallas_call(partial(attn_bwd_kernel, half=half, seq=seq, blk=256), gri...  53.2 us
    pallas_call x1, Pallas kernels, attn_fwd(): pl.pallas_call(partial(attn_fwd_kernel, half=half, seq=seq, blk=256), gri...  35.4 us
    dot_general x4, matrix products, tn(): lax.dot_general(a, b, (((0,), (0,)), ((), ())), preferred_element_type=F32)  30.8 us
    unnamed x34, local copies, waits for them, and re-layouts  24.5 us
  transfers between devices with their start and end apart: 3, of which 2 were waited for; matrix products, arithmetic and copies ran while one was open for 3% of the time, Pallas kernels for 0%

profile of v1, /device:TPU:0, one launch (start us, length us, event | category | flops | bytes accessed | tf_op | source)
XLA Modules:
  0.0 573.0 jit_solution(1646309129272737622)
XLA Ops:
  7.2 2.3 convert_element_type.51
  9.6 0.8 multiply_reduce_fusion
  10.6 0.9 dynamic-update-slice
  11.4 43.2 %all-reduce.1 = f32[9216]{0:T(1024)S(1)} all-reduce(f32[9216]{0:T(1024)S(1)} %dynamic-update-slice), channel_id=1, replica_groups=mesh['dp'=16,'tensor'=2] {'dp','tensor'}, use_global_device_ids=true, to_apply=%add.1 | all-reduce | flops 9216 | bytes 73728
  56.8 1.1 fusion.6.hot
  57.9 1.1 select_convert_fusion.cold
  59.1 78.6 %all-gather.2.cloned.1.call-done = bf16[3,128,96,96]{3,2,1,0:T(8,128)(2,1)} async-done(((bf16[3,8,96,96]{3,2,1,0:T(8,128)(2,1)}), bf16[3,128,96,96]{3,2,1,0:T(8,128)(2,1)}) %all-gather.2.cloned.1.call-update) | async-done | bytes 7077904 | tf_op jit(solution)/shard_map/all_gather | solution.py:456
  137.7 1.2 slice.56
  139.2 1.5 reshape.105.w_out
  140.6 5.6 fusion.12
  146.2 3.0 copy.47
  149.2 6.0 %reshape.109.rest_3_ = bf16[1536,768]{1,0:T(8,128)(2,1)} reshape(bf16[16,96,8,96]{3,2,1,0:T(8,128)(2,1)} %copy.47) | data formatting | bytes 4718592 | tf_op jit(solution)/shard_map/reshape | solution.py:45
  155.1 4.8 copy.46
  159.9 6.4 %reshape.108.rest_2_ = bf16[768,1536]{1,0:T(8,128)(2,1)} reshape(bf16[8,96,16,96]{3,2,1,0:T(8,128)(2,1)} %copy.46) | data formatting | bytes 4718592 | tf_op jit(solution)/shard_map/reshape | solution.py:45
  166.3 1.8 slice.55
  168.1 1.2 copy.43
  169.4 2.9 reshape.104.w_qkv
  172.3 35.4 %attn_fwd.1 = (bf16[2048,1152]{1,0:T(8,128)(2,1)}, bf16[2048,384]{1,0:T(8,128)(2,1)}, f32[2,8,1024]{2,1,0:T(8,128)}, bf16[2048,768]{1,0:T(8,128)(2,1)}) custom-call(bf16[2048,768]{1,0:T(8,128)(2,1)} %tok.3, bf16[768,1152]{1,0:T(8,128)(2,1)} %reshape.104.w_qkv, bf16[384,768]{1,0:T(8,128)(2,1)} %reshape.105.w_out, f32[1,1152]{1,0:T(1,128)} %broadcast_in_dim.38.bias, ...), custom_call_target="tpu_custom_call" | custom-call | tf_op jit(solution)/shard_map/attn_fwd/pallas_call | solution.py:121
  207.6 1.3 broadcast_in_dim.36.valid0.valid1
  208.9 56.8 %feed.1 = (bf16[2048,768]{1,0:T(8,128)(2,1)}, f32[2048,768]{1,0:T(8,128)}, bf16[2048,768]{1,0:T(8,128)(2,1)}, bf16[2048,1536]{1,0:T(8,128)(2,1)}, bf16[2048,768]...) custom-call(bf16[2048,768]{1,0:T(8,128)(2,1)} %tok.3, ...), custom_call_target="tpu_custom_call" | custom-call | tf_op jit(solution)/shard_map/feed/pallas_call | solution.py:381
  265.8 3.3 convolution_convert_fusion.3
  269.1 53.2 %attn_bwd.1 = (bf16[2048,1152]{1,0:T(8,128)(2,1)}, f32[2,8,384]{2,1,0:T(8,128)}, bf16[2048,768]{1,0:T(8,128)(2,1)}) custom-call(bf16[2048,768]{1,0:T(8,128)(2,1)} %get-tuple-element.29.gattn, bf16[2048,1152]{1,0:T(8,128)(2,1)} %get-tuple-element.30.qkv, bf16[2048,384]{1,0:T(8,128)(2,1)} %get-tuple-element.31.ctx, f32[2,8,1024]{2,1,0:T(8,128)} %get-tuple-element.32.lse, ...), custom_call_target="tpu_custom_call" | custom-call | tf_op jit(solution)/shard_map/attn_bwd/pallas_call | solution.py:213
  322.3 8.5 %fusion = bf16[768,1152]{0,1:T(8,128)(2,1)} fusion(bf16[2048,1152]{1,0:T(8,128)(2,1)} %get-tuple-element.34, bf16[2048,768]{1,0:T(8,128)(2,1)} %tok.3), kind=kOutput, calls=%fused_computation.7 | convolution fusion | flops 3624763392 | bytes 9633792 | tf_op jit(solution)/shard_map/dot_general | solution.py:37
  330.9 0.8 reshape.113
  331.7 1.0 copy.49
  332.7 5.1 reshape.111
  337.7 3.4 copy.48
  341.1 9.4 %convolution_convert_fusion.1 = bf16[768,1536]{1,0:T(8,128)(2,1)} fusion(bf16[2048,768]{1,0:T(8,128)(2,1)} %get-tuple-element.35, bf16[2048,1536]{1,0:T(8,128)(2,1)} %get-tuple-element.36), kind=kOutput, calls=%fused_computation.4 | convolution fusion | flops 4833017856 | bytes 11796480 | tf_op jit(solution)/shard_map/dot_general | solution.py:37
  350.5 6.1 %reshape.115 = bf16[8,96,16,96]{3,2,1,0:T(8,128)(2,1)} reshape(bf16[768,1536]{1,0:T(8,128)(2,1)} %convolution_convert_fusion.1) | data formatting | bytes 4718592 | tf_op jit(solution)/shard_map/reshape | solution.py:53
  356.6 4.5 copy.50
  361.1 9.5 %convolution_convert_fusion = bf16[1536,768]{1,0:T(8,128)(2,1)} fusion(bf16[2048,1536]{1,0:T(8,128)(2,1)} %get-tuple-element.37, bf16[2048,768]{1,0:T(8,128)(2,1)S(1)} %copy-done.10), kind=kOutput, calls=%fused_computation.3 | convolution fusion | flops 4833017856 | bytes 11796480 | tf_op jit(solution)/shard_map/dot_general | solution.py:37
  370.6 6.4 %reshape.116 = bf16[16,96,8,96]{3,2,1,0:T(8,128)(2,1)} reshape(bf16[1536,768]{1,0:T(8,128)(2,1)} %convolution_convert_fusion) | data formatting | bytes 4718592 | tf_op jit(solution)/shard_map/reshape | solution.py:53
  377.0 2.7 copy.51
  379.7 0.6 maximum_bitcast_fusion
  380.3 1.3 copy-done.1
  381.6 4.9 copy_bitcast_fusion
  386.5 15.5 %reshape.124 = bf16[128,27648]{1,0:T(8,128)(2,1)} reshape(bf16[128,3,96,96]{3,2,1,0:T(8,128)(2,1)} %copy_bitcast_fusion) | data formatting | bytes 14155776
  404.6 0.8 slice_reduce_fusion.1
  405.6 74.7 %all-reduce.3 = (f32[4608]{0:T(1024)S(1)}, f32[3]{0:T(128)S(1)}, f32[]{:T(128)}) all-reduce(f32[4608]{0:T(1024)S(1)} %pad_maximum_fusion.1, f32[3]{0:T(128)S(1)} %slice_reduce_fusion, f32[]{:T(128)} %fusion.7), channel_id=3, replica_groups=mesh['dp'=16,'tensor'=2] {'dp'}, use_global_device_ids=true, to_apply=%region_4.5.clone | all-reduce | flops 4612 | bytes 36896
  481.5 0.7 divide_subtract_fusion
  482.1 8.2 %convert_add_fusion = f32[2048,768]{1,0:T(8,128)} fusion(bf16[2048,768]{1,0:T(8,128)(2,1)} %collective-permute-done, f32[2048,768]{1,0:T(8,128)} %get-tuple-element.28, bf16[2048,768]{1,0:T(8,128)(2,1)} %get-tuple-element.33), kind=kLoop, calls=%fused_computation.2 | loop fusion | flops 6291456 | bytes 18874368 | tf_op jit(solution)/shard_map/add | solution.py:503
  490.3 61.7 %reduce-scatter.4.cloned.1.call-done = bf16[8,27648]{1,0:T(8,128)(2,1)} async-done(((bf16[128,27648]{1,0:T(8,128)(2,1)}), bf16[8,27648]{1,0:T(8,128)(2,1)}) %reduce-scatter.4.cloned.1.call-update) | async-done | bytes 442384
  552.1 1.6 reshape.125
  553.7 1.2 bitcast_convert_fusion
  554.9 2.8 fusion.3
  557.7 1.5 fusion.4
  559.2 2.8 convolution_subtract_fusion
  562.0 3.8 copy.67
  (59 shorter events, 5.2 us)
Async XLA Ops:
  7.2 552.0 %copy-start = (f32[24,96,96]{2,1,0:T(8,128)S(1)}, f32[24,96,96]{2,1,0:T(8,128)}, u32[]{:S(2)}) copy-start(f32[24,96,96]{2,1,0:T(8,128)} %param.17) | copy-start | bytes 2654212
  7.2 130.5 %all-gather.2.cloned.1.call-start = ((), (), s32[]{:S(2)}) async-start(), calls=%async_computation.1 | async-start | bytes 10027008 | tf_op jit(solution)/shard_map/all_gather | solution.py:456
  9.5 542.6 %reduce-scatter.4.cloned.1.call-start = ((), (), s32[]{:S(2)}) async-start(), calls=%async_computation.2 | async-start | bytes 7520256
  208.9 56.8 %copy-start.4 = (bf16[2048,384]{1,0:T(8,128)(2,1)S(1)}, bf16[2048,384]{1,0:T(8,128)(2,1)}, u32[]{:S(2)}) copy-start(bf16[2048,384]{1,0:T(8,128)(2,1)} %get-tuple-element.31.ctx) | copy-start | bytes 4718596
  356.6 4.5 copy-start.10
  377.0 2.7 copy-start.3
  379.7 1.9 copy-start.1
  402.1 0.7 copy-start.11
  402.1 2.5 copy-start.6
  402.1 2.5 copy-start.7
  402.1 79.4 %copy-start.8 = (f32[288]{0:T(512)S(1)}, f32[288]{0:T(512)}, u32[]{:S(2)}) copy-start(f32[288]{0:T(512)} %param.18) | copy-start | bytes 3460
  402.1 79.4 %copy-start.9 = (f32[288]{0:T(512)S(1)}, f32[288]{0:T(512)}, u32[]{:S(2)}) copy-start(f32[288]{0:T(512)} %param.19) | copy-start | bytes 3460
  402.1 80.0 %collective-permute-start = (bf16[2048,768]{1,0:T(8,128)(2,1)}, bf16[2048,768]{1,0:T(8,128)(2,1)}, u32[]{:S(2)}, u32[]{:S(2)}) collective-permute-start(bf16[2048,768]{1,0:T(8,128)(2,1)} %get-tuple-element.33), channel_id=1, source_target_pairs={{0,1},{1,0},{2,3},{3,2},{4,5},{5,4},{6,7},{7,6},{8,9},{9,8},{10,11... | collective-permute-start | bytes 9437192 | tf_op jit(solution)/shard_map/ppermute | solution.py:503
  553.7 4.0 copy-start.5
  554.9 4.3 copy-start.2
Sparse Core Ops, SparseCore 0:
  11.3 126.3 all-gather.1
  402.2 149.8 reduce-scatter.3

commit v2 on v1

--- a/solution.py
+++ b/solution.py
@@ -266,7 +266,7 @@
     i = pl.program_id(0)
     other = 1 - lax.axis_index("tensor")
     width = tok.shape[1]
-    hidden = w_up.shape[1]
+    hidden = w_down.shape[0]
     chunk = width
 
     def span(t):
@@ -315,7 +315,7 @@
         sums[6:7] += fold(keep * r1 * r1)
         sums[7:8] += fold(keep * att * att)
         for c in range(0, hidden, chunk):
-            u = nn(low, w_up[:, c : c + chunk]) + b_up[:, c : c + chunk]
+            u = nn(low, w_up[c // chunk]) + b_up[:, c : c + chunk]
             both, gauss = erf_parts(u)
             act[:, c : c + chunk] = (0.5 * u * both).astype(BF)
             slope[lax.rem(t, 2), :, c : c + chunk] = (
@@ -348,7 +348,9 @@
             gu = nt(low, w_down[c : c + chunk]) * slope[lax.rem(t, 2), :, c : c + chunk].astype(F32)
             up_sum[0:1, c : c + chunk] += fold(gu)
             gpre[:, c : c + chunk] = gu.astype(BF)
-        send3[span(t)] = nt(gpre[...], w_up[...]).astype(BF)
+        send3[span(t)] = (
+            nt(gpre[:, :chunk], w_up[0]) + nt(gpre[:, chunk:], w_up[1])
+        ).astype(BF)
         copy(2, t).start()
 
     @pl.when(i >= 2)
@@ -372,7 +374,7 @@
 
 def feed(tok, cot, valid, part, w_up, w_down, b_up, vec, blk=256):
     count, width = tok.shape
-    hidden = w_up.shape[1]
+    hidden = w_down.shape[0]
     tiles = count // blk
     lag = lambda n: (lambda i: (jnp.clip(i - n, 0, tiles - 1), 0))
     whole = lambda shape: pl.BlockSpec(shape, lambda i: (0,) * len(shape))
@@ -388,7 +390,7 @@
             pl.BlockSpec((blk, LANES), lag(1)),
             wide(0),
             pl.BlockSpec(memory_space=pl.ANY),
-            whole((width, hidden)),
+            whole(w_up.shape),
             whole((hidden, width)),
             whole((1, hidden)),
             whole((8, width)),
@@ -432,6 +434,543 @@
 
 def feed_kernel_entry(tok, cot, valid0, valid1, *rest, tiles, blk):
     feed_kernel(tok, cot, Both(valid0, valid1), *rest, tiles=tiles, blk=blk)
+
+
+PLANE = 4
+DEPTH = 4
+UP, DOWN, ALONG_X, ALONG_Y = 0, 1, 2, 3
+
+
+def where_am_i():
+    dp = lax.axis_index("dp")
+    return dp, dp // PLANE, lax.rem(dp, PLANE)
+
+
+def flip(xy, bit):
+    step = 1 if bit == ALONG_X else 2
+    side = lax.rem(xy // step, 2)
+    return xy + step - 2 * step * side
+
+
+def toward(direction):
+    dp, z, xy = where_am_i()
+    if direction == UP:
+        return dp + PLANE
+    if direction == DOWN:
+        return dp - PLANE
+    return z * PLANE + flip(xy, direction)
+
+
+def greet():
+    dp, z, xy = where_am_i()
+    barrier = pltpu.get_barrier_semaphore()
+    other = 1 - lax.axis_index("tensor")
+
+    def tell(device):
+        pl.semaphore_signal(barrier, inc=1, device_id=device, device_id_type=MESH)
+
+    tell({"tensor": other})
+    tell({"dp": toward(ALONG_X)})
+    tell({"dp": toward(ALONG_Y)})
+    pl.when(z < DEPTH - 1)(lambda: tell({"dp": toward(UP)}))
+    pl.when(z > 0)(lambda: tell({"dp": toward(DOWN)}))
+    inner = jnp.logical_and(z < DEPTH - 1, z > 0)
+    pl.semaphore_wait(barrier, jnp.where(inner, 5, 4))
+
+
+class Gather:
+    def __init__(self, kinds, send_sem, recv_sem):
+        self.kinds = kinds
+        self.send_sem, self.recv_sem = send_sem, recv_sem
+        self.dp, self.z, self.xy = where_am_i()
+        self.started = []
+
+    def copy(self, c, direction, origin, part):
+        place, first, rows = self.kinds[c]
+        ref = place(origin)
+        if part == 1:
+            ref = ref.at[pl.ds(0, first)]
+        if part == 2:
+            ref = ref.at[pl.ds(first, rows - first)]
+        slot = origin if part != 2 else DEPTH * PLANE + origin // PLANE
+        lane = direction if part == 0 else direction + 2
+        return pltpu.make_async_remote_copy(
+            src_ref=ref,
+            dst_ref=ref,
+            send_sem=self.send_sem.at[c, lane, origin],
+            recv_sem=self.recv_sem.at[c, slot],
+            device_id={"dp": toward(direction)},
+            device_id_type=MESH,
+        )
+
+    def send(self, ok, c, direction, origin, part=0):
+        start = lambda: self.copy(c, direction, origin, part).start()
+        start() if ok is None else pl.when(ok)(start)
+        self.started.append((ok, c, direction, origin, part))
+
+    def levels(self, k):
+        if k == 0:
+            return [(None, self.z)]
+        below, above = self.z - k, self.z + k
+        return [(below >= 0, below), (above < DEPTH, above)]
+
+    def along(self, c, k):
+        for ok, level in self.levels(k):
+            origin = level * PLANE + self.xy
+            up, down = self.z < DEPTH - 1, self.z > 0
+            if k == 0:
+                self.send(up, c, UP, origin)
+                self.send(down, c, DOWN, origin)
+            else:
+                pl.when(ok)(lambda: self.copy(c, ALONG_X, origin, 0).wait_recv())
+                from_below = level < self.z
+                self.send(ok & from_below & up, c, UP, origin)
+                self.send(ok & jnp.logical_not(from_below) & down, c, DOWN, origin)
+            self.send(ok, c, ALONG_X, origin)
+            self.send(ok, c, ALONG_Y, origin)
+
+    def across(self, c, k):
+        first, rows = self.kinds[c][1:]
+        for ok, level in self.levels(k):
+            for came, onward, part in ((ALONG_X, ALONG_Y, 1), (ALONG_Y, ALONG_X, 2)):
+                origin = level * PLANE + flip(self.xy, came)
+                wait = lambda came=came, origin=origin: self.copy(c, came, origin, 0).wait_recv()
+                wait() if ok is None else pl.when(ok)(wait)
+                if part == 1 or rows > first:
+                    self.send(ok, c, onward, origin, part if rows > first else 3)
+
+    def last(self, c):
+        first, rows = self.kinds[c][1:]
+        diag = flip(flip(self.xy, ALONG_X), ALONG_Y)
+        for level in range(DEPTH):
+            origin = level * PLANE + diag
+            if rows > first:
+                self.copy(c, ALONG_Y, origin, 1).wait_recv()
+                self.copy(c, ALONG_X, origin, 2).wait_recv()
+            else:
+                self.copy(c, ALONG_Y, origin, 3).wait_recv()
+
+    def sent(self):
+        for ok, c, direction, origin, part in self.started:
+            lane = max(direction, ALONG_X) if part else direction
+            wait = lambda: self.copy(c, lane, origin, part).wait_send()
+            wait() if ok is None else pl.when(ok)(wait)
+        self.started = []
+
+
+class Scatter:
+    def __init__(self, kinds, bufs, send_sem, recv_sem):
+        self.kinds, self.bufs = kinds, bufs
+        self.send_sem, self.recv_sem = send_sem, recv_sem
+        self.dp, self.z, self.xy = where_am_i()
+        self.started = []
+
+    def level(self, k):
+        return jnp.where(self.z < DEPTH // 2, DEPTH - 1 - k, k)
+
+    def copy(self, c, what, src, dst, direction, level):
+        return pltpu.make_async_remote_copy(
+            src_ref=src,
+            dst_ref=dst,
+            send_sem=self.send_sem.at[c, what, level],
+            recv_sem=self.recv_sem.at[c, what, level],
+            device_id={"dp": toward(direction)},
+            device_id_type=MESH,
+        )
+
+    def term(self, c, column, level):
+        return self.kinds[c][0](level * PLANE + column)
+
+    def parts(self, c, what, level):
+        place, first, rows, _ = self.kinds[c]
+        got_a, got_b, got_x, got_y, got_up, got_down, put_x, put_y, put_z = self.bufs[c]
+        diag = flip(flip(self.xy, ALONG_X), ALONG_Y)
+        if what == 0:
+            return self.term(c, diag, level).at[pl.ds(0, first)], got_a.at[level], ALONG_Y
+        if what == 1:
+            return self.term(c, diag, level).at[pl.ds(first, rows - first)], got_b.at[level], ALONG_X
+        if what == 2:
+            return put_x.at[level], got_x.at[level], ALONG_X
+        if what == 3:
+            return put_y.at[level], got_y.at[level], ALONG_Y
+        if what == 4:
+            return put_z.at[level], got_up.at[level], UP
+        return put_z.at[level], got_down.at[level], DOWN
+
+    def start(self, c, what, level):
+        src, dst, direction = self.parts(c, what, level)
+        self.copy(c, what, src, dst, direction, level).start()
+
+    def wait(self, c, what, level, sent=False):
+        src, dst, direction = self.parts(c, what, level)
+        copy = self.copy(c, what, src, dst, ALONG_X, level)
+        copy.wait_send() if sent else copy.wait_recv()
+
+    def first(self, c, k):
+        place, first, rows, _ = self.kinds[c]
+        self.start(c, 0, self.level(k))
+        if rows > first:
+            self.start(c, 1, self.level(k))
+
+    def second(self, c, k):
+        place, first, rows, _ = self.kinds[c]
+        level = self.level(k)
+        got_a, got_b, _, _, _, _, put_x, put_y, _ = self.bufs[c]
+        a, b = pl.ds(0, first), pl.ds(first, rows - first)
+        own_x = self.term(c, flip(self.xy, ALONG_X), level)
+        own_y = self.term(c, flip(self.xy, ALONG_Y), level)
+        self.wait(c, 0, level)
+        add = lambda p, q: (p.astype(F32) + q.astype(F32)).astype(put_x.dtype)
+        put_x[level, a] = add(own_x[a], got_a[level])
+        if rows > first:
+            put_x[level, b] = own_x[b]
+        self.start(c, 2, level)
+        if rows > first:
+            self.wait(c, 1, level)
+            put_y[level, b] = add(own_y[b], got_b[level])
+        put_y[level, a] = own_y[a]
+        self.start(c, 3, level)
+
+    def third(self, c, k):
+        level = self.level(k)
+        _, _, got_x, got_y, got_up, got_down, _, _, put_z = self.bufs[c]
+        total = self.kinds[c][3]
+        self.wait(c, 2, level)
+        self.wait(c, 3, level)
+        own = self.term(c, self.xy, level)
+        here = own[...].astype(F32) + got_x[level].astype(F32) + got_y[level].astype(F32)
+
+        @pl.when(level == self.z)
+        def _():
+            total[...] = here
+
+        for what, beyond, more, got in (
+            (4, level > self.z, self.z > 0, got_up),
+            (5, level < self.z, self.z < DEPTH - 1, got_down),
+        ):
+
+            @pl.when(jnp.logical_and(beyond, jnp.logical_not(more)))
+            def _():
+                put_z[level] = here.astype(put_z.dtype)
+                self.start(c, what, level)
+
+            @pl.when(jnp.logical_and(beyond, more))
+            def _():
+                self.wait(c, what, level)
+                put_z[level] = (here + got[level].astype(F32)).astype(put_z.dtype)
+                self.start(c, what, level)
+
+    def last(self, c):
+        got_up, got_down = self.bufs[c][4:6]
+        total = self.kinds[c][3]
+
+        @pl.when(self.z > 0)
+        def _():
+            self.wait(c, 4, self.z)
+            total[...] += got_up[self.z].astype(F32)
+
+        @pl.when(self.z < DEPTH - 1)
+        def _():
+            self.wait(c, 5, self.z)
+            total[...] += got_down[self.z].astype(F32)
+
+    def sent(self, c):
+        place, first, rows, _ = self.kinds[c]
+        for level in range(DEPTH):
+            self.wait(c, 0, level, True)
+            if rows > first:
+                self.wait(c, 1, level, True)
+            self.wait(c, 2, level, True)
+            self.wait(c, 3, level, True)
+            pl.when(level > self.z)(lambda: self.wait(c, 4, level, True))
+            pl.when(level < self.z)(lambda: self.wait(c, 5, level, True))
+
+
+GATHER_SLOTS = DEPTH * PLANE + DEPTH
+KINDS = 3
+
+
+def gather_kernel(mat, vec, w0, w1, w2, vecs, send_sem, recv_sem, swap_sem, *, edge, per):
+    half, width = w0.shape[2], w1.shape[2]
+    dp, z, xy = where_am_i()
+    own = lax.axis_index("tensor")
+    wide = per * edge
+    greet()
+
+    def place0(d):
+        return w0.at[d // PLANE, pl.ds(pl.multiple_of(lax.rem(d, PLANE) * 2 * edge, 2 * edge), 2 * edge)]
+
+    def place1(d):
+        return w1.at[lax.rem(d, 2), pl.ds(pl.multiple_of(d // 2 * edge, edge), edge)]
+
+    def place2(d):
+        return w2.at[pl.ds(pl.multiple_of(d * edge, edge), edge)]
+
+    def place3(d):
+        return vecs.at[own, d]
+
+    gather = Gather(
+        [
+            (place3, vec.shape[0], vec.shape[0]),
+            (place0, edge, 2 * edge),
+            (place1, edge // 2, edge),
+            (place2, edge // 2, edge),
+        ],
+        send_sem,
+        recv_sem,
+    )
+    place3(dp)[...] = vec[...]
+    gather.along(0, 0)
+    mine0, mine1, mine2 = place0(dp), place1(dp), place2(dp)
+    for j in range(per):
+        at = pl.ds(j % (per // 2) * edge, edge)
+        mine0[pl.ds(j // (per // 2) * edge, edge), at] = mat[j].astype(BF)
+    gather.along(1, 0)
+    for j in range(per):
+        mine1[:, pl.ds(j * edge, edge)] = mat[per + j].astype(BF)
+        mine2[:, pl.ds(j * edge, edge)] = mat[2 * per + j].astype(BF)
+    for k in range(1, DEPTH):
+        gather.along(0, k)
+        gather.across(0, k - 1)
+        gather.along(1, k)
+        gather.across(1, k - 1)
+    gather.across(0, DEPTH - 1)
+    gather.across(1, DEPTH - 1)
+    gather.along(2, 0)
+    for k in range(1, DEPTH):
+        gather.along(2, k)
+        gather.across(2, k - 1)
+    gather.across(2, DEPTH - 1)
+    gather.along(3, 0)
+    gather.last(0)
+    swap = pltpu.make_async_remote_copy(
+        src_ref=vecs.at[own],
+        dst_ref=vecs.at[own],
+        send_sem=swap_sem.at[0],
+        recv_sem=swap_sem.at[1],
+        device_id={"tensor": 1 - own},
+        device_id_type=MESH,
+    )
+    swap.start()
+    gather.last(1)
+    gather.last(2)
+    for k in range(1, DEPTH):
+        gather.along(3, k)
+        gather.across(3, k - 1)
+    gather.across(3, DEPTH - 1)
+    gather.last(3)
+    gather.sent()
+    swap.wait()
+
+
+def gather_weights(mat, vec):
+    per, edge = mat.shape[0] // KINDS, mat.shape[-1]
+    wide = per * edge
+    count = DEPTH * PLANE
+    vmem = pl.BlockSpec(memory_space=pltpu.VMEM)
+    return pl.pallas_call(
+        partial(gather_kernel, edge=edge, per=per),
+        in_specs=[vmem] * 2,
+        out_specs=[vmem] * 4,
+        out_shape=[
+            jax.ShapeDtypeStruct((4, wide, wide // 2), BF),
+            jax.ShapeDtypeStruct((2, wide, wide), BF),
+            jax.ShapeDtypeStruct((2 * wide, wide), BF),
+            jax.ShapeDtypeStruct((2, count, *vec.shape), F32),
+        ],
+        scratch_shapes=[
+            pltpu.SemaphoreType.DMA((4, 6, count)),
+            pltpu.SemaphoreType.DMA((4, GATHER_SLOTS)),
+            pltpu.SemaphoreType.DMA((2,)),
+        ],
+        compiler_params=params(collective_id=2, has_side_effects=True),
+        name="gather_weights",
+    )(mat, vec)
+
+
+SCATTER_BUFS = 9
+
+
+def scatter_kernel(
+    g0, g1, g2, gv, master, left, right, root_l, root_r,
+    grads, left_new, right_new, mat_new, vec_total, total0, total1, *rest, edge, per,
+):
+    bufs, (send_sem, recv_sem) = rest[:-2], rest[-2:]
+    bufs = [bufs[c * SCATTER_BUFS : (c + 1) * SCATTER_BUFS] for c in range(4)]
+
+    def place0(d):
+        return g0.at[d]
+
+    def place1(d):
+        return g1.at[lax.rem(d, 2), pl.ds(pl.multiple_of(d // 2 * edge, edge), edge)]
+
+    def place2(d):
+        return g2.at[pl.ds(pl.multiple_of(d * edge, edge), edge)]
+
+    def place3(d):
+        return gv.at[d]
+
+    kinds = [
+        (place3, gv.shape[1], gv.shape[1], vec_total),
+        (place2, edge // 2, edge, total1),
+        (place1, edge // 2, edge, total1),
+        (place0, edge, 2 * edge, total0),
+    ]
+    scatter = Scatter(kinds, bufs, send_sem, recv_sem)
+    greet()
+
+    def block(number, grad):
+        low = grad.astype(BF)
+        grads[number] = grad
+        left_new[number] = DECAY * left[number] + (1.0 - DECAY) * nt(low, low)
+        right_new[number] = DECAY * right[number] + (1.0 - DECAY) * tn(low, low)
+        turned = nn(root_l[number].astype(BF), low).astype(BF)
+        mat_new[number] = master[number] - STEP_RATE * nn(turned, root_r[number].astype(BF))
+
+    def finish(c):
+        if c == 3:
+            for j in range(per):
+                block(j, total0[pl.ds(j // (per // 2) * edge, edge), pl.ds(j % (per // 2) * edge, edge)])
+        else:
+            base = (3 - c) * per
+            for j in range(per):
+                block(base + j, total1[:, pl.ds(j * edge, edge)])
+
+    for c in range(4):
+        for k in range(DEPTH):
+            scatter.first(c, k)
+        for k in range(DEPTH):
+            scatter.second(c, k)
+        if c > 0:
+            for k in range(DEPTH):
+                scatter.third(c - 1, k)
+            scatter.last(c - 1)
+            if c > 1:
+                finish(c - 1)
+    for k in range(DEPTH):
+        scatter.third(3, k)
+    scatter.last(3)
+    finish(3)
+    for c in range(4):
+        scatter.sent(c)
+
+
+def scatter_grads(g0, g1, g2, gv, master, left, right, root_l, root_r):
+    per, edge = master.shape[0] // KINDS, master.shape[-1]
+    wide = per * edge
+    vmem = pl.BlockSpec(memory_space=pltpu.VMEM)
+    rows = gv.shape[1]
+
+    def bufs(first, full, cols, kind):
+        a, b = (DEPTH, first, cols), (DEPTH, max(full - first, first), cols)
+        f = (DEPTH, full, cols)
+        return [pltpu.VMEM(s, kind) for s in (a, b, f, f, f, f, f, f, f)]
+
+    return pl.pallas_call(
+        partial(scatter_kernel, edge=edge, per=per),
+        in_specs=[vmem] * 9,
+        out_specs=[vmem] * 5,
+        out_shape=[jax.ShapeDtypeStruct(master.shape, F32)] * 4
+        + [jax.ShapeDtypeStruct(gv.shape[1:], F32)],
+        scratch_shapes=[
+            pltpu.VMEM((2 * edge, wide // 2), F32),
+            pltpu.VMEM((edge, wide), F32),
+            *bufs(rows, rows, gv.shape[2], F32),
+            *bufs(edge // 2, edge, wide, BF),
+            *bufs(edge // 2, edge, wide, BF),
+            *bufs(edge, 2 * edge, wide // 2, BF),
+            pltpu.SemaphoreType.DMA((4, 6, DEPTH)),
+            pltpu.SemaphoreType.DMA((4, 6, DEPTH)),
+        ],
+        compiler_params=params(collective_id=3, has_side_effects=True),
+        name="scatter_grads",
+    )(g0, g1, g2, gv, master, left, right, root_l, root_r)
+
+
+def far_weights(mat_master, vec_master, width):
+    half = width // 2
+    edge = mat_master.shape[-1]
+    local = mat_master.astype(BF).reshape(KINDS, -1, edge, edge)
+    blocks = lax.all_gather(local, "dp", axis=1, tiled=True)
+    kind_count = blocks.shape[1]
+    quarter = kind_count // 4
+    grid_model = width // edge
+    grid_half = half // edge
+    grid_hidden = kind_count // grid_model
+    w_project = (
+        blocks[0, : 3 * quarter]
+        .reshape(3, grid_model, grid_half, edge, edge)
+        .transpose(1, 3, 0, 2, 4)
+        .reshape(width, 3 * half)
+    )
+    w_out = unblock(blocks[0, 3 * quarter :], grid_half, grid_model)
+    w_up = unblock(blocks[1], grid_model, grid_hidden).reshape(width, -1, width)
+    w_down = unblock(blocks[2], grid_hidden, grid_model)
+    shard = vec_master.shape[0]
+    every = lax.all_gather(vec_master, ("dp", "tensor"), axis=0, tiled=True)
+    halves = every.reshape(-1, 2, shard).transpose(1, 0, 2).reshape(2, 12, half)
+    return w_project, w_out, w_up.transpose(1, 0, 2), w_down, halves
+
+
+def near_weights(mat_master, vec_master, width):
+    half = width // 2
+    edge = mat_master.shape[-1]
+    shard = vec_master.shape[0]
+    rows = -(-shard // LANES)
+    vec = jnp.pad(vec_master, (0, 8 * LANES - shard)).reshape(8, LANES)
+    w0, w_up, w_down, vecs = gather_weights(mat_master, vec)
+    halves = vecs[:, :, :rows].reshape(2, -1, rows * LANES)[:, :, :shard].reshape(2, 12, half)
+    w_project = w0[:3].transpose(1, 0, 2).reshape(width, 3 * half)
+    w_out = w0[3].reshape(-1, 2, edge, half).transpose(0, 2, 1, 3).reshape(half, width)
+    return w_project, w_out, w_up, w_down, halves
+
+
+def far_step(grads, state):
+    grad_project, grad_out_weight, grad_up, grad_down, vec_local, sizes = grads
+    mat_master, mat_left, mat_right, root_left, root_right = state
+    edge = mat_master.shape[-1]
+    width, half = grad_project.shape[0], grad_project.shape[1] // 3
+    project_blocks = (
+        grad_project.reshape(width // edge, edge, 3, half // edge, edge)
+        .transpose(2, 0, 3, 1, 4)
+        .reshape(-1, edge, edge)
+    )
+    attention_blocks = jnp.concatenate([project_blocks, to_blocks(grad_out_weight, edge)], axis=0)
+    owned = lax.psum_scatter(
+        jnp.stack([attention_blocks, to_blocks(grad_up, edge), to_blocks(grad_down, edge)]),
+        "dp",
+        scatter_dimension=1,
+        tiled=True,
+    )
+    vec_grads = lax.psum_scatter(vec_local, "dp", scatter_dimension=0, tiled=True)
+    mat_grads = owned.astype(F32).reshape(-1, edge, edge)
+    left_new = DECAY * mat_left + (1.0 - DECAY) * jnp.einsum("bij,bkj->bik", mat_grads, mat_grads)
+    right_new = DECAY * mat_right + (1.0 - DECAY) * jnp.einsum("bji,bjk->bik", mat_grads, mat_grads)
+    turned = jnp.einsum("bij,bjk->bik", root_left, mat_grads)
+    turned = jnp.einsum("bij,bjk->bik", turned, root_right)
+    mat_new = mat_master - STEP_RATE * turned
+    return mat_grads, left_new, right_new, mat_new, vec_grads, lax.psum(sizes, "dp")
+
+
+def near_step(grads, state):
+    grad_project, grad_out_weight, grad_up, grad_down, vec_local, sizes = grads
+    edge = state[0].shape[-1]
+    width, half = grad_project.shape[0], grad_project.shape[1] // 3
+    count = DEPTH * PLANE
+    shard = vec_local.shape[0] // count
+    room = 8 * LANES
+    project = grad_project.reshape(PLANE, 2 * edge, 3, half).transpose(2, 0, 1, 3)
+    out = grad_out_weight.reshape(PLANE, edge, 2, half).transpose(0, 2, 1, 3)
+    g0 = jnp.concatenate(
+        [project.reshape(3 * PLANE, 2 * edge, half), out.reshape(PLANE, 2 * edge, half)]
+    )
+    g1 = grad_up.reshape(width, 2, width).transpose(1, 0, 2)
+    spread = jnp.broadcast_to(sizes[None], (count, sizes.shape[0]))
+    gv = jnp.concatenate([vec_local.reshape(count, shard), spread], axis=1)
+    gv = jnp.pad(gv, ((0, 0), (0, room - gv.shape[1]))).reshape(count, 8, LANES)
+    *mats, vec_total = scatter_grads(g0, g1, grad_down, gv, *state)
+    flat = vec_total.reshape(-1)
+    return *mats, flat[:shard], flat[shard : shard + sizes.shape[0]]
 
 
 def body(
@@ -452,25 +991,10 @@
     seq = tokens.shape[0] // row_count
     edge = mat_master.shape[-1]
     own_index = lax.axis_index("tensor")
-    local = mat_master.astype(BF).reshape(3, -1, edge, edge)
-    blocks = lax.all_gather(local, "dp", axis=1, tiled=True)
-    kind_count = blocks.shape[1]
-    quarter = kind_count // 4
-    grid_model = width // edge
-    grid_half = half // edge
-    grid_hidden = kind_count // grid_model
-    w_project = (
-        blocks[0, : 3 * quarter]
-        .reshape(3, grid_model, grid_half, edge, edge)
-        .transpose(1, 3, 0, 2, 4)
-        .reshape(width, 3 * half)
-    )
-    w_out = unblock(blocks[0, 3 * quarter :], grid_half, grid_model)
-    w_up = unblock(blocks[1], grid_model, grid_hidden)
-    w_down = unblock(blocks[2], grid_hidden, grid_model)
     shard = vec_master.shape[0]
-    every = lax.all_gather(vec_master, ("dp", "tensor"), axis=0, tiled=True)
-    halves = every.reshape(-1, 2, shard).transpose(1, 0, 2).reshape(2, 12, half)
+    fast = lax.axis_size("dp") == DEPTH * PLANE and mat_master.shape[0] == KINDS * width // edge
+    weights = near_weights if fast else far_weights
+    w_project, w_out, w_up, w_down, halves = weights(mat_master, vec_master, width)
     own = lax.dynamic_index_in_dim(halves, own_index, 0, keepdims=False)
     shared = jnp.concatenate([halves[0, 6:], halves[1, 6:]], axis=1)
     bias_up = own[2:6].reshape(1, -1)
@@ -502,32 +1026,16 @@
     swap = [(0, 1), (1, 0)]
     input_grad = gr1 + part_in.astype(F32) + lax.ppermute(part_in, "tensor", swap).astype(F32)
 
-    squares, count = lax.psum((jnp.sum(sums[6:9], axis=1), jnp.sum(keep)), "dp")
-    stream_rms = jnp.sqrt(squares / (count * width))
-
-    project_blocks = (
-        grad_project.reshape(grid_model, edge, 3, grid_half, edge)
-        .transpose(2, 0, 3, 1, 4)
-        .reshape(3 * quarter, edge, edge)
-    )
-    attention_blocks = jnp.concatenate([project_blocks, to_blocks(grad_out_weight, edge)], axis=0)
-    feed_blocks = jnp.stack([to_blocks(grad_up, edge), to_blocks(grad_down, edge)])
+    sizes = jnp.concatenate([jnp.sum(sums[6:9], axis=1), jnp.sum(keep)[None]])
     bias_pair = jnp.sum(bias_sums, axis=0)
     shared_sums = lax.dynamic_slice_in_dim(sums[:6], own_index * half, half, axis=1)
     vec_local = jnp.concatenate([bias_pair[:2].reshape(-1), up_sum[0], shared_sums.reshape(-1)])
-    owned = lax.psum_scatter(
-        jnp.concatenate([attention_blocks[None], feed_blocks], axis=0),
-        "dp",
-        scatter_dimension=1,
-        tiled=True,
-    )
-    vec_grads = lax.psum_scatter(vec_local, "dp", scatter_dimension=0, tiled=True)
-    mat_grads = owned.astype(F32).reshape(-1, edge, edge)
-    left_new = DECAY * mat_left + (1.0 - DECAY) * jnp.einsum("bij,bkj->bik", mat_grads, mat_grads)
-    right_new = DECAY * mat_right + (1.0 - DECAY) * jnp.einsum("bji,bjk->bik", mat_grads, mat_grads)
-    turned = jnp.einsum("bij,bjk->bik", root_left, mat_grads)
-    turned = jnp.einsum("bij,bjk->bik", turned, root_right)
-    mat_new = mat_master - STEP_RATE * turned
+    step = near_step if fast else far_step
+    mat_grads, left_new, right_new, mat_new, vec_grads, sizes = step(
+        (grad_project, grad_out_weight, grad_up, grad_down, vec_local, sizes),
+        (mat_master, mat_left, mat_right, root_left, root_right),
+    )
+    stream_rms = jnp.sqrt(sizes[:3] / (sizes[3] * width))
     second_new = DECAY * vec_second + (1.0 - DECAY) * vec_grads * vec_grads
     vec_new = vec_master - VEC_RATE * vec_grads / (jnp.sqrt(second_new) + VEC_EPS)
     return (

time: 582 us -> 415 us (0.71)
  Pallas kernels: 145 us -> 322 us
  waiting for transfers between devices: 140 us -> 0.01 us
  blocking collectives: 118 us -> 0 us
  local copies, waits for them, and re-layouts: 92 us -> 37.1 us
  between operations: 16.1 us -> 1.81 us
  matrix products: 37.8 us -> 30.6 us
    pallas_call x0 -> x2, Pallas kernels: none -> 167 us  [the longest x1 92.5 us: scatter_grads(): pl.pallas_call(partial(scatter_kernel, edge=edge, per=per), in_specs=[vme...]
    unnamed x2 -> x0, blocking collectives: 118 us -> none
    all_gather x1 -> x0, waiting for transfers between devices: 78.6 us -> none  [body(): blocks = lax.all_gather(local, 'dp', axis=1, tiled=True)]
    unnamed x3 -> x0, waiting for transfers between devices: 61.8 us -> none
    reshape x14 -> x9, local copies, waits for them, and re-layouts: 46.8 us -> 11.4 us  [the longest x1 3.29 us: near_step(): grad_project.reshape(PLANE, 2 * edge, 3, half).transpose(2, 0, 1, 3)]
    unnamed x34 -> x47, local copies, waits for them, and re-layouts: 24.5 us -> 9.36 us
    pallas_call x1, Pallas kernels: 53.2 us -> 61.4 us  [attn_bwd(): pl.pallas_call(partial(attn_bwd_kernel, half=half, seq=seq, blk=256), gri...]
    dot_general x3 -> x0, matrix products: 7.04 us -> none  [the longest x1 2.75 us: body(): turned = jnp.einsum('bij,bjk->bik', turned, root_right)]
  transfers between devices with their start and end apart: 3 -> 1, of which waited for: 2 -> 0; matrix products, arithmetic and copies ran while one was open for 3% -> 13% of each run, Pallas kernels for 0% -> 23%
where the time goes in v2:
time: 415 us; the launch traced here: 410 us
  Pallas kernels  322 us (78%)
  local copies, waits for them, and re-layouts  37.1 us (9%)
  matrix products  30.6 us (7%)
  other arithmetic  18.6 us (4%)
    pallas_call x1, Pallas kernels, scatter_grads(): pl.pallas_call(partial(scatter_kernel, edge=edge, per=per), in_specs=[vme...  92.5 us
    pallas_call x1, Pallas kernels, gather_weights(): pl.pallas_call(partial(gather_kernel, edge=edge, per=per), in_specs=[vmem...  74.7 us
    pallas_call x1, Pallas kernels, attn_bwd(): pl.pallas_call(partial(attn_bwd_kernel, half=half, seq=seq, blk=256), gri...  61.4 us
    pallas_call x1, Pallas kernels, feed(): pl.pallas_call(partial(feed_kernel_entry, tiles=tiles, blk=blk), grid=(ti...  58.4 us
    pallas_call x1, Pallas kernels, attn_fwd(): pl.pallas_call(partial(attn_fwd_kernel, half=half, seq=seq, blk=256), gri...  34.9 us
    dot_general x4, matrix products, tn(): lax.dot_general(a, b, (((0,), (0,)), ((), ())), preferred_element_type=F32)  30.6 us
    unnamed x47, local copies, waits for them, and re-layouts  9.36 us
  transfers between devices with their start and end apart: 1, of which 0 were waited for; matrix products, arithmetic and copies ran while one was open for 13% of the time, Pallas kernels for 23%

profile of v2, /device:TPU:0, one launch (start us, length us, event | category | flops | bytes accessed | tf_op | source)
XLA Modules:
  0.0 410.4 jit_solution(256129764493336103)
XLA Ops:
  0.7 0.8 multiply_reduce_fusion
  1.6 1.1 fusion.2.hot
  2.7 1.3 pad_bitcast_fusion.1.vec
  4.0 74.7 %gather_weights.1 = (bf16[4,768,384]{2,1,0:T(8,128)(2,1)}, bf16[2,768,768]{2,1,0:T(8,128)(2,1)}, bf16[1536,768]{1,0:T(8,128)(2,1)}, f32[2,16,8,128]{3,2,1,0:T(8,128)}) custom-call(f32[24,96,96]{2,1,0:T(8,128)} %master.1, f32[8,128]{1,0:T(8,128)} %pad_bitcast_fusion.1.vec), custom_call_target="tpu_custom_call" | custom-call | tf_op jit(solution)/shard_map/gather_weights/pallas_call | solution.py:771
  78.7 2.0 slice.55
  80.7 1.7 slice_bitcast_fusion
  82.4 1.1 select_convert_fusion.cold
  83.6 0.6 slice_bitcast_fusion.2
  84.3 0.6 broadcast_in_dim.44.bias
  84.9 0.6 copy.44
  85.5 0.9 copy.33
  86.5 2.2 copy.35.w_qkv
  88.7 0.5 copy.34
  89.2 0.9 copy.43
  90.1 0.6 select_maximum_fusion.rest_5_
  90.7 34.9 %attn_fwd.1 = (bf16[2048,1152]{1,0:T(8,128)(2,1)}, bf16[2048,384]{1,0:T(8,128)(2,1)}, f32[2,8,1024]{2,1,0:T(8,128)}, bf16[2048,768]{1,0:T(8,128)(2,1)}) custom-call(bf16[2048,768]{1,0:T(8,128)(2,1)} %tok.3, bf16[768,1152]{1,0:T(8,128)(2,1)} %copy.35.w_qkv, bf16[384,768]{1,0:T(8,128)(2,1)} %bitcast.51, f32[1,1152]{1,0:T(1,128)} %broadcast_in_dim.44.bias, ...), custom_call_target="tpu_custom_call" | custom-call | tf_op jit(solution)/shard_map/attn_fwd/pallas_call | solution.py:121
  125.6 1.3 broadcast_in_dim.42.valid0.valid1
  126.9 58.4 %feed.1 = (bf16[2048,768]{1,0:T(8,128)(2,1)}, f32[2048,768]{1,0:T(8,128)}, bf16[2048,768]{1,0:T(8,128)(2,1)}, bf16[2048,1536]{1,0:T(8,128)(2,1)}, bf16[2048,768]...) custom-call(bf16[2048,768]{1,0:T(8,128)(2,1)} %tok.3, ...), custom_call_target="tpu_custom_call" | custom-call | tf_op jit(solution)/shard_map/feed/pallas_call | solution.py:383
  185.3 61.4 %attn_bwd.1 = (bf16[2048,1152]{1,0:T(8,128)(2,1)}, f32[2,8,384]{2,1,0:T(8,128)}, bf16[2048,768]{1,0:T(8,128)(2,1)}) custom-call(bf16[2048,768]{1,0:T(8,128)(2,1)} %get-tuple-element.42.gattn, bf16[2048,1152]{1,0:T(8,128)(2,1)} %get-tuple-element.43.qkv, bf16[2048,384]{1,0:T(8,128)(2,1)} %get-tuple-element.44.ctx, f32[2,8,1024]{2,1,0:T(8,128)} %get-tuple-element.45.lse, ...), custom_call_target="tpu_custom_call" | custom-call | tf_op jit(solution)/shard_map/attn_bwd/pallas_call | solution.py:213
  246.7 0.4 collective-permute-start
  247.2 0.6 fusion.3
  247.8 4.7 %convolution_convert_fusion.3 = bf16[384,768]{1,0:T(8,128)(2,1)} fusion(bf16[2048,384]{1,0:T(8,128)(2,1)} %get-tuple-element.44.ctx, bf16[2048,768]{1,0:T(8,128)(2,1)} %get-tuple-element.42.gattn), kind=kOutput, calls=%fused_computation.7 | convolution fusion | flops 1208254464 | bytes 5308416 | tf_op jit(solution)/shard_map/dot_general | solution.py:37
  252.5 0.1 slice_reduce_fusion
  252.7 7.5 %fusion = bf16[768,1152]{0,1:T(8,128)(2,1)} fusion(bf16[2048,1152]{1,0:T(8,128)(2,1)} %get-tuple-element.47, bf16[2048,768]{1,0:T(8,128)(2,1)S(1)} %copy-done), kind=kOutput, calls=%fused_computation.4 | convolution fusion | flops 3624763392 | bytes 9633792 | tf_op jit(solution)/shard_map/dot_general | solution.py:37
  260.1 0.9 slice_reduce_fusion.1
  261.2 0.7 pad_maximum_fusion.4
  261.9 1.8 reshape.108
  263.9 2.2 copy.37
  266.1 0.6 copy.45
  266.7 3.3 reshape.106
  270.0 1.5 copy.38
  271.6 1.0 copy-done.17
  272.6 9.1 %convolution_convert_fusion.1 = bf16[768,1536]{1,0:T(8,128)(2,1)} fusion(bf16[2048,768]{1,0:T(8,128)(2,1)S(1)} %copy-done.17, bf16[2048,1536]{1,0:T(8,128)(2,1)} %get-tuple-element.49), kind=kOutput, calls=%fused_computation.2 | convolution fusion | flops 4833017856 | bytes 11796480 | tf_op jit(solution)/shard_map/dot_general | solution.py:37
  281.7 2.8 copy.40
  284.5 2.5 copy.41
  287.0 3.3 pad_maximum_fusion.g0
  290.3 9.3 %convolution_convert_fusion.g2 = bf16[1536,768]{1,0:T(8,128)(2,1)} fusion(bf16[2048,1536]{1,0:T(8,128)(2,1)} %get-tuple-element.50, bf16[2048,768]{1,0:T(8,128)(2,1)S(1)} %copy-done.16), kind=kOutput, calls=%fused_computation.1 | convolution fusion | flops 4833017856 | bytes 11796480 | tf_op jit(solution)/shard_map/dot_general | solution.py:37
  299.6 92.5 %scatter_grads.1 = (f32[24,96,96]{2,1,0:T(8,128)}, f32[24,96,96]{2,1,0:T(8,128)}, f32[24,96,96]{2,1,0:T(8,128)}, f32[24,96,96]{2,1,0:T(8,128)}, f32[8,128]{1,0:T(8,128)}) custom-call(bf16[16,192,384]{2,1,0:T(8,128)(2,1)} %pad_maximum_fusion.g0, bf16[2,768,768]{2,1,0:T(8,128)(2,1)} %bitcast.46, bf16[1536,768]{1,0:T(8,128)(2,1)} %convolution_convert_fusion.g2, ...), custom_call_target="tpu_custom_call" | custom-call | tf_op jit(solution)/shard_map/scatter_grads/pallas_call | solution.py:869
  392.1 1.3 slice.69
  394.0 1.3 divide_sqrt_fusion
  395.3 1.3 divide_subtract_fusion
  396.6 7.4 %convert_add_fusion = f32[2048,768]{1,0:T(8,128)} fusion(bf16[2048,768]{1,0:T(8,128)(2,1)} %collective-permute-done, f32[2048,768]{1,0:T(8,128)} %get-tuple-element.41, bf16[2048,768]{1,0:T(8,128)(2,1)S(1)} %copy-done.1), kind=kLoop, calls=%fused_computation | loop fusion | flops 6291456 | bytes 18874368 | tf_op jit(solution)/shard_map/add | solution.py:1027
  404.0 1.7 copy.53
  405.7 0.4 copy-done.8
  406.1 1.0 copy.54
  407.1 1.0 copy.55
  408.1 1.0 copy.56
  409.2 1.0 copy.57
  (58 shorter events, 0.6 us)
Async XLA Ops:
  78.7 4.8 %copy-start.11 = (f32[2,16,8,128]{3,2,1,0:T(8,128)S(1)}, f32[2,16,8,128]{3,2,1,0:T(8,128)}, u32[]{:S(2)}) copy-start(f32[2,16,8,128]{3,2,1,0:T(8,128)} %get-tuple-element.36) | copy-start | bytes 393220
  86.5 2.2 copy-start.3
  86.5 3.6 copy-start.9
  86.5 3.6 copy-start.10
  246.7 149.9 %collective-permute-start = (bf16[2048,768]{1,0:T(8,128)(2,1)}, bf16[2048,768]{1,0:T(8,128)(2,1)}, u32[]{:S(2)}, u32[]{:S(2)}) collective-permute-start(bf16[2048,768]{1,0:T(8,128)(2,1)} %get-tuple-element.46), channel_id=1, source_target_pairs={{0,1},{1,0},{2,3},{3,2},{4,5},{5,4},{6,7},{7,6},{8,9},{9,8},{10,11... | collective-permute-start | bytes 9437192 | tf_op jit(solution)/shard_map/ppermute | solution.py:1027
  247.8 4.8 %copy-start.12 = (f32[16,768]{1,0:T(8,128)S(1)}, f32[16,768]{1,0:T(8,128)}, u32[]{:S(2)}) copy-start(f32[16,768]{1,0:T(8,128)} %get-tuple-element.54) | copy-start | bytes 147460
  247.8 4.9 %copy-start = (bf16[2048,768]{1,0:T(8,128)(2,1)S(1)}, bf16[2048,768]{1,0:T(8,128)(2,1)}, u32[]{:S(2)}) copy-start(bf16[2048,768]{1,0:T(8,128)(2,1)} %tok.3) | copy-start | bytes 9437188
  252.7 8.4 %copy-start.13 = (f32[2,8,384]{2,1,0:T(8,128)S(1)}, f32[2,8,384]{2,1,0:T(8,128)}, u32[]{:S(2)}) copy-start(f32[2,8,384]{2,1,0:T(8,128)} %get-tuple-element.52) | copy-start | bytes 73732
  260.1 3.7 copy-start.4
  270.0 2.5 copy-start.17
  287.0 3.3 copy-start.16
  299.6 95.7 %copy-start.14 = (f32[288]{0:T(512)S(1)}, f32[288]{0:T(512)}, u32[]{:S(2)}) copy-start(f32[288]{0:T(512)} %param.18) | copy-start | bytes 3460
  299.6 95.7 %copy-start.15 = (f32[288]{0:T(512)S(1)}, f32[288]{0:T(512)}, u32[]{:S(2)}) copy-start(f32[288]{0:T(512)} %param.19) | copy-start | bytes 3460
  299.6 97.0 %copy-start.1 = (bf16[2048,768]{1,0:T(8,128)(2,1)S(1)}, bf16[2048,768]{1,0:T(8,128)(2,1)}, u32[]{:S(2)}) copy-start(bf16[2048,768]{1,0:T(8,128)(2,1)} %get-tuple-element.46) | copy-start | bytes 9437188
  396.6 7.4 %copy-start.2 = (bf16[2048,768]{1,0:T(8,128)(2,1)S(1)}, bf16[2048,768]{1,0:T(8,128)(2,1)}, u32[]{:S(2)}) copy-start(bf16[2048,768]{1,0:T(8,128)(2,1)} %get-tuple-element.77) | copy-start | bytes 9437188
  404.0 2.1 copy-start.8
  404.0 3.1 copy-start.7
  406.1 2.0 copy-start.6
  406.1 3.0 copy-start.5

commit v3 on v2

v3 whole, which is shorter than its diff:
```python
from functools import partial
import math

import jax
import jax.numpy as jnp
from jax import lax
from jax.experimental import pallas as pl
from jax.experimental.pallas import tpu as pltpu
from jax.sharding import PartitionSpec as P

HD = 64
LN_EPS = 1e-12
BIG = 1e30
FLOOR = -1e29
DECAY = 0.5
STEP_RATE = 1.0
VEC_RATE = 0.1
VEC_EPS = 1e-08
INV_ROOT_TWO = 1.0 / math.sqrt(2.0)
INV_ROOT_TWO_PI = 1.0 / math.sqrt(2.0 * math.pi)
BF = jnp.bfloat16
F32 = jnp.float32
LANES = 128
VMEM_LIMIT = 60 * 2**20
MESH = pl.DeviceIdType.MESH


def nn(a, b):
    return lax.dot_general(a, b, (((1,), (0,)), ((), ())), preferred_element_type=F32)


def nt(a, b):
    return lax.dot_general(a, b, (((1,), (1,)), ((), ())), preferred_element_type=F32)


def tn(a, b):
    return lax.dot_general(a, b, (((0,), (0,)), ((), ())), preferred_element_type=F32)


def unblock(blocks, grid_rows, grid_cols):
    edge = blocks.shape[-1]
    return (
        blocks.reshape(grid_rows, grid_cols, edge, edge)
        .transpose(0, 2, 1, 3)
        .reshape(grid_rows * edge, grid_cols * edge)
    )


def to_blocks(matrix, edge):
    grid_rows = matrix.shape[0] // edge
    grid_cols = matrix.shape[1] // edge
    return (
        matrix.reshape(grid_rows, edge, grid_cols, edge)
        .transpose(0, 2, 1, 3)
        .reshape(grid_rows * grid_cols, edge, edge)
    )


def erf_parts(u):
    z = jnp.abs(u) * INV_ROOT_TWO
    gauss = jnp.exp(-z * z)
    t = 1.0 / (1.0 + 0.3275911 * z)
    poly = t * (
        0.254829592
        + t * (-0.284496736 + t * (1.421413741 + t * (-1.453152027 + t * 1.061405429)))
    )
    tail = poly * gauss
    return jnp.where(u >= 0.0, 2.0 - tail, tail), gauss


def params(**kw):
    return pltpu.CompilerParams(vmem_limit_bytes=VMEM_LIMIT, **kw)


def low_lanes(shape):
    return lax.broadcasted_iota(jnp.int32, shape, 1) < HD


def attend(qkv, ctx, hot, cold, rows, half, between=None):
    blk = hot.shape[0]
    low = low_lanes((blk, LANES))
    lane = lax.broadcasted_iota(jnp.int32, (blk, LANES), 1)
    stats = jnp.zeros((blk, LANES), F32)
    for pair in range(half // LANES):
        if between is not None:
            between(pair)
        cols = pl.ds(pair * LANES, LANES)
        q_pair = qkv[rows, cols] * jnp.asarray(HD**-0.5, BF)
        k_aug = jnp.concatenate([qkv[:, pl.ds(half + pair * LANES, LANES)], cold], axis=1)
        v_pair = qkv[:, pl.ds(2 * half + pair * LANES, LANES)]
        outs = []
        for side in range(2):
            own = low if side == 0 else jnp.logical_not(low)
            q_aug = jnp.concatenate([jnp.where(own, q_pair, 0), hot], axis=1)
            s = nt(q_aug, k_aug)
            top = jnp.maximum(jnp.max(s, axis=1, keepdims=True), FLOOR)
            e = jnp.exp(s - top)
            total = jnp.maximum(jnp.sum(e, axis=1, keepdims=True), 0.5)
            outs.append(nn(e.astype(BF), v_pair) / total)
            stats = jnp.where(lane == 2 * pair + side, top + jnp.log(total), stats)
        ctx[rows, cols] = jnp.where(low, outs[0], outs[1]).astype(BF)
    return stats


def attn_fwd_kernel(
    tok, w_qkv, w_out, bias, hot, cold, qkv, ctx, lse, part, *, half, seq, blk
):
    qkv[...] = (nn(tok[...], w_qkv[...]) + bias[...]).astype(BF)

    def step(index, carry):
        rows = pl.ds(pl.multiple_of(index * blk, blk), blk)
        stats = attend(qkv, ctx, hot[0, rows, :], cold[0], rows, half)
        lse[0, :, rows] = stats.T[: lse.shape[1]]
        return carry

    lax.fori_loop(0, seq // blk, step, 0)
    part[...] = nn(ctx[...], w_out[...]).astype(BF)


def attn_fwd(tok, w_qkv, w_out, bias, hot, cold, rows, seq):
    width = tok.shape[1]
    half = width // 2
    stat_rows = -(-(half // HD) // 8) * 8
    whole = lambda shape: pl.BlockSpec(shape, lambda r: (0,) * len(shape))
    return pl.pallas_call(
        partial(attn_fwd_kernel, half=half, seq=seq, blk=256),
        grid=(rows,),
        in_specs=[
            pl.BlockSpec((seq, width), lambda r: (r, 0)),
            whole((width, 3 * half)),
            whole((half, width)),
            whole((1, 3 * half)),
            pl.BlockSpec((1, seq, LANES), lambda r: (r, 0, 0)),
            pl.BlockSpec((1, seq, LANES), lambda r: (r, 0, 0)),
        ],
        out_specs=[
            pl.BlockSpec((seq, 3 * half), lambda r: (r, 0)),
            pl.BlockSpec((seq, half), lambda r: (r, 0)),
            pl.BlockSpec((1, stat_rows, seq), lambda r: (r, 0, 0)),
            pl.BlockSpec((seq, width), lambda r: (r, 0)),
        ],
        out_shape=[
            jax.ShapeDtypeStruct((rows * seq, 3 * half), BF),
            jax.ShapeDtypeStruct((rows * seq, half), BF),
            jax.ShapeDtypeStruct((rows, stat_rows, seq), F32),
            jax.ShapeDtypeStruct((rows * seq, width), BF),
        ],
        compiler_params=params(),
        name="attn_fwd",
    )(tok, w_qkv, w_out, bias, hot, cold)


def attend_back(
    qkv, gctx, lse, centre, hot, cold, rows, half, gq_out, dk, dv, between=None
):
    blk = hot.shape[0]
    low = low_lanes((blk, LANES))
    scale = jnp.asarray(HD**-0.5, BF)
    sums = []
    for pair in range(half // LANES):
        if between is not None:
            between(pair)
        cols = pl.ds(pair * LANES, LANES)
        q_pair = qkv[rows, cols] * scale
        g_pair = gctx[rows, cols]
        k_pair = qkv[:, pl.ds(half + pair * LANES, LANES)]
        k_aug = jnp.concatenate([k_pair, cold], axis=1)
        v_pair = qkv[:, pl.ds(2 * half + pair * LANES, LANES)]
        outs = []
        dk_new = dk[:, cols]
        dv_new = dv[:, cols]
        for side in range(2):
            head = pl.ds(2 * pair + side, 1)
            own = low if side == 0 else jnp.logical_not(low)
            q_own = jnp.where(own, q_pair, 0)
            g_own = jnp.where(own, g_pair, 0)
            s = nt(k_aug, jnp.concatenate([q_own, hot], axis=1))
            p = jnp.exp(s - lse[head, rows])
            gp = nt(v_pair, g_own)
            gs = (p * (gp - centre[head, rows])).astype(BF)
            dv_new = dv_new + nn(p.astype(BF), g_own)
            dk_new = dk_new + nn(gs, q_own)
            outs.append(tn(gs, k_pair))
        dk[:, cols] = dk_new
        dv[:, cols] = dv_new
        gq = jnp.where(low, outs[0], outs[1]) * HD**-0.5
        gq_out[:, cols] = gq.astype(BF)
        sums.append(fold(gq))
    return jnp.concatenate(sums, axis=1)


def context_grad(gattn, ctx, w_out, gctx, centre, half):
    gctx[...] = nt(gattn[...], w_out[...]).astype(BF)
    prod = gctx[...].astype(F32) * ctx[...].astype(F32)
    picks = (
        lax.broadcasted_iota(jnp.int32, (8, half), 0)
        == lax.broadcasted_iota(jnp.int32, (8, half), 1) // HD
    ).astype(F32)
    centre[...] = lax.dot_general(
        picks, prod, (((1,), (1,)), ((), ())),
        preferred_element_type=F32, precision=lax.Precision.HIGHEST,
    )


def attn_bwd_kernel(
    gattn, qkv, ctx, lse, w_qkv, w_out, hot, cold, gqkv, sums, part, gctx, centre, dk, dv,
    *, half, seq, blk,
):
    context_grad(gattn, ctx, w_out, gctx, centre, half)
    dk[...] = jnp.zeros_like(dk)
    dv[...] = jnp.zeros_like(dv)

    def step(index, gq_sum):
        rows = pl.ds(pl.multiple_of(index * blk, blk), blk)
        out = gqkv.at[rows, pl.ds(0, half)]
        return gq_sum + attend_back(
            qkv, gctx, lse.at[0], centre, hot[0, rows, :], cold[0], rows, half, out, dk, dv
        )

    gq_sum = lax.fori_loop(0, seq // blk, step, jnp.zeros((1, half), F32))
    gqkv[:, pl.ds(half, half)] = dk[...].astype(BF)
    gqkv[:, pl.ds(2 * half, half)] = dv[...].astype(BF)
    sums[0, 0:1, :] = gq_sum
    sums[0, 1:2, :] = fold(dv[...])
    part[...] = nt(gqkv[...], w_qkv[...]).astype(BF)


def attn_bwd(gattn, qkv, ctx, lse, w_qkv, w_out, hot, cold, rows, seq):
    width = gattn.shape[1]
    half = width // 2
    whole = lambda shape: pl.BlockSpec(shape, lambda r: (0,) * len(shape))
    return pl.pallas_call(
        partial(attn_bwd_kernel, half=half, seq=seq, blk=256),
        grid=(rows,),
        in_specs=[
            pl.BlockSpec((seq, width), lambda r: (r, 0)),
            pl.BlockSpec((seq, 3 * half), lambda r: (r, 0)),
            pl.BlockSpec((seq, half), lambda r: (r, 0)),
            pl.BlockSpec((1, lse.shape[1], seq), lambda r: (r, 0, 0)),
            whole((width, 3 * half)),
            whole((half, width)),
            pl.BlockSpec((1, seq, LANES), lambda r: (r, 0, 0)),
            pl.BlockSpec((1, seq, LANES), lambda r: (r, 0, 0)),
        ],
        out_specs=[
            pl.BlockSpec((seq, 3 * half), lambda r: (r, 0)),
            pl.BlockSpec((1, 8, half), lambda r: (r, 0, 0)),
            pl.BlockSpec((seq, width), lambda r: (r, 0)),
        ],
        out_shape=[
            jax.ShapeDtypeStruct((rows * seq, 3 * half), BF),
            jax.ShapeDtypeStruct((rows, 8, half), F32),
            jax.ShapeDtypeStruct((rows * seq, width), BF),
        ],
        scratch_shapes=[
            pltpu.VMEM((seq, half), BF),
            pltpu.VMEM((8, seq), F32),
            pltpu.VMEM((seq, half), F32),
            pltpu.VMEM((seq, half), F32),
        ],
        compiler_params=params(),
        name="attn_bwd",
    )(gattn, qkv, ctx, lse, w_qkv, w_out, hot, cold)


def mean_last(x):
    return jnp.mean(x, axis=-1, keepdims=True)


def norm_back(grad, normal, inverse, gain):
    scaled = grad * gain
    return inverse * (scaled - mean_last(scaled) - normal * mean_last(scaled * normal))


def fold(x):
    return jnp.sum(x, axis=0, keepdims=True)


def feed_kernel(
    tok, cot, valid0, valid1, part, part_all, w_up, w_down, flat,
    out, r1_grad, gattn, grad_up, grad_down, sums, up_sum,
    got1, send, got2, got3, normal1, inv1, grad2, act, hid, gfeed, gpre, send_sem, recv_sem,
    *, tiles, blk,
):
    i = pl.program_id(0)
    me = lax.axis_index("tensor")
    other = 1 - me
    width = tok.shape[1]
    half = width // 2
    hidden = w_down.shape[0]
    chunk = width

    def span(t):
        return pl.ds(pl.multiple_of(t * blk, blk), blk)

    def copy(stage, t):
        return pltpu.make_async_remote_copy(
            src_ref=(part_all, send, send)[stage].at[span(t)],
            dst_ref=(got1, got2, got3)[stage].at[span(t)],
            send_sem=send_sem.at[stage, t],
            recv_sem=recv_sem.at[stage, t],
            device_id={"tensor": other},
            device_id_type=MESH,
        )

    @pl.when(i == 0)
    def _():
        barrier = pltpu.get_barrier_semaphore()
        pl.semaphore_signal(barrier, inc=1, device_id={"tensor": other}, device_id_type=MESH)
        pl.semaphore_wait(barrier, 1)
        for t in range(tiles):
            copy(0, t).start()
        sums[...] = jnp.zeros_like(sums)
        up_sum[...] = jnp.zeros_like(up_sum)

    def shared(piece):
        at = pl.ds(piece * half, half)
        return jnp.concatenate([flat[0:1, at], flat[1:2, at]], axis=1)

    bias_out, bias_down, gain1, shift1, gain2, shift2 = [shared(6 + n) for n in range(6)]
    b_up = flat[pl.ds(me, 1), pl.ds(2 * half, hidden)]

    @pl.when(i < tiles)
    def _():
        t = i
        slot = lax.rem(t, 3)
        copy(0, t).wait()
        keep = valid0[:, :1]
        att = part[...].astype(F32) + got1[span(t)].astype(F32) + bias_out
        r1 = tok[...].astype(F32) + att
        centred = r1 - mean_last(r1)
        inverse = lax.rsqrt(mean_last(centred * centred) + LN_EPS)
        normal = centred * inverse
        normal1[slot] = normal
        inv1[slot] = jnp.broadcast_to(inverse, (blk, LANES))
        low = (normal * gain1 + shift1).astype(BF)
        hid[span(t)] = low
        sums[6:7] += fold(keep * r1 * r1)
        sums[7:8] += fold(keep * att * att)
        for c in range(0, hidden, chunk):
            at = pl.ds(c, chunk)
            u = nn(low, w_up[c // chunk]) + b_up[:, c : c + chunk]
            both, gauss = erf_parts(u)
            act[span(t), at] = (0.5 * u * both).astype(BF)
            gpre[span(t), at] = (0.5 * both + u * gauss * INV_ROOT_TWO_PI).astype(BF)
        send[span(t)] = nn(act[span(t)], w_down[...]).astype(BF)
        copy(1, t).start()

    @pl.when((i >= 1) & (i <= tiles))
    def _():
        t = i - 1
        copy(1, t).wait()
        keep = valid1[:, :1]
        feed = send[span(t)].astype(F32) + got2[span(t)].astype(F32) + bias_down
        r2 = normal1[lax.rem(t, 3)] * gain1 + shift1 + feed
        centred = r2 - mean_last(r2)
        inverse = lax.rsqrt(mean_last(centred * centred) + LN_EPS)
        normal = centred * inverse
        out[...] = (normal * gain2 + shift2).astype(BF)
        g = cot[...].astype(F32) * keep
        gr = norm_back(g, normal, inverse, gain2)
        grad2[lax.rem(t, 2)] = gr
        sums[1:2] += fold(gr)
        sums[4:5] += fold(g * normal)
        sums[5:6] += fold(g)
        sums[8:9] += fold(keep * feed * feed)
        sums[9:10, :LANES] += fold(valid1[...])
        low = gr.astype(BF)
        gfeed[span(t)] = low
        total = jnp.zeros((blk, width), F32)
        for c in range(0, hidden, chunk):
            at = pl.ds(c, chunk)
            gu = nt(low, w_down[at]) * gpre[span(t), at].astype(F32)
            up_sum[0:1, at] += fold(gu)
            gu_low = gu.astype(BF)
            gpre[span(t), at] = gu_low
            total = total + nt(gu_low, w_up[c // chunk])
        send[span(t)] = total.astype(BF)
        copy(2, t).start()

    @pl.when(i == tiles + 1)
    def _():
        for c in range(0, hidden, half):
            grad_down[pl.ds(c, half)] = tn(act[:, c : c + half], gfeed[...]).astype(BF)

    @pl.when(i >= 2)
    def _():
        t = i - 2
        slot = lax.rem(t, 3)
        copy(2, t).wait()
        gh = grad2[lax.rem(t, 2)] + send[span(t)].astype(F32) + got3[span(t)].astype(F32)
        normal = normal1[slot]
        gr = norm_back(gh, normal, inv1[slot][:, :1], gain1)
        sums[0:1] += fold(gr)
        sums[2:3] += fold(gh * normal)
        sums[3:4] += fold(gh)
        r1_grad[...] = gr
        gattn[...] = gr.astype(BF)

    @pl.when(i == tiles + 1)
    def _():
        for c in range(0, hidden, chunk):
            for r in range(0, width, half):
                grad_up[c // chunk, pl.ds(r, half)] = tn(
                    hid[:, r : r + half], gpre[:, c : c + chunk]
                ).astype(BF)


def once(shape):
    return pl.BlockSpec(shape, lambda *i: (0,) * len(shape), pipeline_mode=pl.Buffered(1))


def feed(tok, cot, valid, part, w_up, w_down, flat, blk=256):
    count, width = tok.shape
    hidden = w_down.shape[0]
    tiles = count // blk
    lag = lambda n: (lambda i: (jnp.clip(i - n, 0, tiles - 1), 0))
    wide = lambda n: pl.BlockSpec((blk, width), lag(n))
    return pl.pallas_call(
        partial(feed_kernel, tiles=tiles, blk=blk),
        grid=(tiles + 2,),
        in_specs=[
            wide(0),
            wide(1),
            pl.BlockSpec((blk, LANES), lag(0)),
            pl.BlockSpec((blk, LANES), lag(1)),
            wide(0),
            pl.BlockSpec(memory_space=pl.ANY),
            once(w_up.shape),
            once((hidden, width)),
            once(flat.shape),
        ],
        out_specs=[
            wide(1), wide(2), wide(2), once(w_up.shape), once((hidden, width)),
            once((16, width)), once((8, hidden)),
        ],
        out_shape=[
            jax.ShapeDtypeStruct((count, width), BF),
            jax.ShapeDtypeStruct((count, width), F32),
            jax.ShapeDtypeStruct((count, width), BF),
            jax.ShapeDtypeStruct(w_up.shape, BF),
            jax.ShapeDtypeStruct((hidden, width), BF),
            jax.ShapeDtypeStruct((16, width), F32),
            jax.ShapeDtypeStruct((8, hidden), F32),
        ],
        scratch_shapes=[
            *[pltpu.VMEM((count, width), BF) for _ in range(4)],
            pltpu.VMEM((3, blk, width), F32),
            pltpu.VMEM((3, blk, LANES), F32),
            pltpu.VMEM((2, blk, width), F32),
            pltpu.VMEM((count, hidden), BF),
            pltpu.VMEM((count, width), BF),
            pltpu.VMEM((count, width), BF),
            pltpu.VMEM((count, hidden), BF),
            pltpu.SemaphoreType.DMA((3, tiles)),
            pltpu.SemaphoreType.DMA((3, tiles)),
        ],
        compiler_params=params(collective_id=1, has_side_effects=True),
        name="feed",
    )(tok, cot, valid, valid, part, part, w_up, w_down, flat)


PLANE = 4
DEPTH = 4
UP, DOWN, ALONG_X, ALONG_Y = 0, 1, 2, 3


def where_am_i():
    dp = lax.axis_index("dp")
    return dp, dp // PLANE, lax.rem(dp, PLANE)


def flip(xy, bit):
    step = 1 if bit == ALONG_X else 2
    side = lax.rem(xy // step, 2)
    return xy + step - 2 * step * side


def toward(direction):
    dp, z, xy = where_am_i()
    if direction == UP:
        return dp + PLANE
    if direction == DOWN:
        return dp - PLANE
    return z * PLANE + flip(xy, direction)


def greet():
    dp, z, xy = where_am_i()
    barrier = pltpu.get_barrier_semaphore()
    other = 1 - lax.axis_index("tensor")

    def tell(device):
        pl.semaphore_signal(barrier, inc=1, device_id=device, device_id_type=MESH)

    tell({"tensor": other})
    tell({"dp": toward(ALONG_X)})
    tell({"dp": toward(ALONG_Y)})
    pl.when(z < DEPTH - 1)(lambda: tell({"dp": toward(UP)}))
    pl.when(z > 0)(lambda: tell({"dp": toward(DOWN)}))
    inner = jnp.logical_and(z < DEPTH - 1, z > 0)
    pl.semaphore_wait(barrier, jnp.where(inner, 5, 4))


class Gather:
    def __init__(self, kinds, send_sem, recv_sem):
        self.kinds = kinds
        self.send_sem, self.recv_sem = send_sem, recv_sem
        self.dp, self.z, self.xy = where_am_i()

    def copy(self, c, direction, origin, part):
        place, first, rows = self.kinds[c]
        ref = place(origin)
        if part == 1:
            ref = ref.at[pl.ds(0, first)]
        if part == 2:
            ref = ref.at[pl.ds(first, rows - first)]
        slot = origin if part != 2 else DEPTH * PLANE + origin // PLANE
        lane = direction if part == 0 else direction + 2
        return pltpu.make_async_remote_copy(
            src_ref=ref,
            dst_ref=ref,
            send_sem=self.send_sem.at[c, lane, origin],
            recv_sem=self.recv_sem.at[c, slot],
            device_id={"dp": toward(direction)},
            device_id_type=MESH,
        )

    def send(self, ok, c, direction, origin, part=0):
        start = lambda: self.copy(c, direction, origin, part).start()
        start() if ok is None else pl.when(ok)(start)

    def levels(self, k):
        if k == 0:
            return [(None, self.z)]
        below, above = self.z - k, self.z + k
        return [(below >= 0, below), (above < DEPTH, above)]

    def along(self, c, k):
        for ok, level in self.levels(k):
            origin = level * PLANE + self.xy
            up, down = self.z < DEPTH - 1, self.z > 0
            if k == 0:
                self.send(up, c, UP, origin)
                self.send(down, c, DOWN, origin)
            else:
                pl.when(ok)(lambda: self.copy(c, ALONG_X, origin, 0).wait_recv())
                from_below = level < self.z
                self.send(ok & from_below & up, c, UP, origin)
                self.send(ok & jnp.logical_not(from_below) & down, c, DOWN, origin)
            self.send(ok, c, ALONG_X, origin)
            self.send(ok, c, ALONG_Y, origin)

    def across(self, c, k):
        first, rows = self.kinds[c][1:]
        for ok, level in self.levels(k):
            for came, onward, part in ((ALONG_X, ALONG_Y, 1), (ALONG_Y, ALONG_X, 2)):
                origin = level * PLANE + flip(self.xy, came)
                wait = lambda came=came, origin=origin: self.copy(c, came, origin, 0).wait_recv()
                wait() if ok is None else pl.when(ok)(wait)
                if part == 1 or rows > first:
                    self.send(ok, c, onward, origin, part if rows > first else 3)

    def last(self, c):
        first, rows = self.kinds[c][1:]
        diag = flip(flip(self.xy, ALONG_X), ALONG_Y)
        for level in range(DEPTH):
            origin = level * PLANE + diag
            if rows > first:
                self.copy(c, ALONG_Y, origin, 1).wait_recv()
                self.copy(c, ALONG_X, origin, 2).wait_recv()
            else:
                self.copy(c, ALONG_Y, origin, 3).wait_recv()

    def sent(self):
        for c, (_, first, rows) in enumerate(self.kinds):
            left = lambda *what: self.copy(c, *what).wait_send()
            for level in range(DEPTH):
                here = level * PLANE + self.xy
                up = jnp.logical_and(level <= self.z, self.z < DEPTH - 1)
                down = jnp.logical_and(level >= self.z, self.z > 0)
                pl.when(up)(lambda: left(UP, here, 0))
                pl.when(down)(lambda: left(DOWN, here, 0))
                left(ALONG_X, here, 0)
                left(ALONG_Y, here, 0)
                beside = level * PLANE + flip(self.xy, ALONG_X)
                left(ALONG_Y, beside, 1 if rows > first else 3)
                if rows > first:
                    left(ALONG_X, level * PLANE + flip(self.xy, ALONG_Y), 2)


class Scatter:
    def __init__(self, kinds, send_sem, recv_sem):
        self.kinds = kinds
        self.send_sem, self.recv_sem = send_sem, recv_sem
        self.dp, self.z, self.xy = where_am_i()

    def term(self, c, column, level):
        return self.kinds[c][0](level * PLANE + column)

    def copy(self, c, what, level, direction=None):
        first, rows, _, got = self.kinds[c][1:]
        column, way = (
            (flip(flip(self.xy, ALONG_X), ALONG_Y), ALONG_Y),
            (flip(flip(self.xy, ALONG_X), ALONG_Y), ALONG_X),
            (flip(self.xy, ALONG_X), ALONG_X),
            (flip(self.xy, ALONG_Y), ALONG_Y),
            (self.xy, UP),
            (self.xy, DOWN),
        )[what]
        src = self.term(c, column, level)
        if what == 0:
            src = src.at[pl.ds(0, first)]
        if what == 1:
            src = src.at[pl.ds(first, rows - first)]
        return pltpu.make_async_remote_copy(
            src_ref=src,
            dst_ref=got[what].at[level],
            send_sem=self.send_sem.at[c, what, level],
            recv_sem=self.recv_sem.at[c, what, level],
            device_id={"dp": toward(way if direction is None else direction)},
            device_id_type=MESH,
        )

    def start(self, c, what, level):
        self.copy(c, what, level).start()

    def came(self, c, what, level):
        self.copy(c, what, level, ALONG_X).wait_recv()

    def left(self, c, what, level):
        self.copy(c, what, level, ALONG_X).wait_send()

    def split(self, c):
        return self.kinds[c][2] > self.kinds[c][1]

    def first(self, c, level):
        self.start(c, 0, level)
        if self.split(c):
            self.start(c, 1, level)

    def second(self, c, level):
        first, rows, _, got = self.kinds[c][1:]
        a, b = pl.ds(0, first), pl.ds(first, rows - first)
        own_x = self.term(c, flip(self.xy, ALONG_X), level)
        own_y = self.term(c, flip(self.xy, ALONG_Y), level)
        add = lambda p, q: (p.astype(F32) + q.astype(F32)).astype(p.dtype)
        self.came(c, 0, level)
        own_x[a] = add(own_x[a], got[0][level])
        self.start(c, 2, level)
        if self.split(c):
            self.came(c, 1, level)
            own_y[b] = add(own_y[b], got[1][level])
        self.start(c, 3, level)

    def third(self, c, level):
        total, got = self.kinds[c][3:]
        own = self.term(c, self.xy, level)
        self.came(c, 2, level)
        self.came(c, 3, level)
        here = own[...].astype(F32) + got[2][level].astype(F32) + got[3][level].astype(F32)

        @pl.when(level == self.z)
        def _():
            total[...] = here

        for what, beyond, more in (
            (4, level > self.z, self.z > 0),
            (5, level < self.z, self.z < DEPTH - 1),
        ):

            @pl.when(jnp.logical_and(beyond, jnp.logical_not(more)))
            def _():
                own[...] = here.astype(own.dtype)
                self.start(c, what, level)

            @pl.when(jnp.logical_and(beyond, more))
            def _():
                self.came(c, what, level)
                own[...] = (here + got[what][level].astype(F32)).astype(own.dtype)
                self.start(c, what, level)

    def last(self, c):
        total, got = self.kinds[c][3:]
        for what, more in ((4, self.z > 0), (5, self.z < DEPTH - 1)):

            @pl.when(more)
            def _():
                self.came(c, what, self.z)
                total[...] += got[what][self.z].astype(F32)

    def sent(self, c):
        for level in range(DEPTH):
            self.left(c, 0, level)
            if self.split(c):
                self.left(c, 1, level)
            self.left(c, 2, level)
            self.left(c, 3, level)
            pl.when(level > self.z)(lambda: self.left(c, 4, level))
            pl.when(level < self.z)(lambda: self.left(c, 5, level))


def landing(first, rows, cols, kind):
    halves = [(DEPTH, first, cols), (DEPTH, max(rows - first, first), cols)]
    return [pltpu.VMEM(shape, kind) for shape in halves + [(DEPTH, rows, cols)] * 4]


GATHER_SLOTS = DEPTH * PLANE + DEPTH
KINDS = 3
VEC_ROWS = 8


def step_at(position, pair):
    i, j = divmod(position, 3)
    return pl.program_id(0) == i if pair == j else None


def play(schedule, pair):
    for position, work in schedule:
        now = step_at(position, pair)
        if now is not None:

            @pl.when(now)
            def _():
                work()


def front_kernel(
    tok, hot, cold, mat, vec,
    qkv, ctx, lse, part, flat, wk_out, w_out, w1_out, w2_out,
    wk, w1, w2, vecs, wo, send_sem, recv_sem, swap_sem, out_sem,
    *, edge, per, seq, blk, steps,
):
    i = pl.program_id(0)
    width = tok.shape[1]
    half = width // 2
    shard = vec.shape[1]
    own = lax.axis_index("tensor")

    def place0(d):
        rows = pl.ds(pl.multiple_of(lax.rem(d, PLANE) * 2 * edge, 2 * edge), 2 * edge)
        return wk.at[rows, pl.ds(pl.multiple_of(d // PLANE * half, half), half)]

    def place1(d):
        return w1.at[lax.rem(d, 2), pl.ds(pl.multiple_of(d // 2 * edge, edge), edge)]

    def place2(d):
        return w2.at[pl.ds(pl.multiple_of(d * edge, edge), edge)]

    def place3(d):
        return vecs.at[own, d]

    gather = Gather(
        [
            (place3, VEC_ROWS, VEC_ROWS),
            (place0, edge, 2 * edge),
            (place1, edge // 2, edge),
            (place2, edge // 2, edge),
        ],
        send_sem,
        recv_sem,
    )
    swap = pltpu.make_async_remote_copy(
        src_ref=vecs.at[own],
        dst_ref=vecs.at[own],
        send_sem=swap_sem.at[0],
        recv_sem=swap_sem.at[1],
        device_id={"tensor": 1 - own},
        device_id_type=MESH,
    )
    saves = [
        pltpu.make_async_copy(src, dst, out_sem.at[n])
        for n, (src, dst) in enumerate(((wk, wk_out), (wo, w_out), (w1, w1_out), (w2, w2_out)))
    ]
    dp = gather.dp

    @pl.when(i == 0)
    def _():
        mine0, mine1, mine2 = place0(dp), place1(dp), place2(dp)
        for j in range(per):
            at = pl.ds(j % (per // 2) * edge, edge)
            mine0[pl.ds(j // (per // 2) * edge, edge), at] = mat[j].astype(BF)
        place3(dp)[...] = jnp.zeros(vecs.shape[2:], F32)
        place3(dp)[0:1, pl.ds(0, shard)] = vec[...]
        greet()
        gather.along(1, 0)
        gather.along(0, 0)
        for j in range(per):
            mine1[:, pl.ds(j * edge, edge)] = mat[per + j].astype(BF)
            mine2[:, pl.ds(j * edge, edge)] = mat[2 * per + j].astype(BF)
        for k in range(1, DEPTH):
            gather.along(1, k)
            gather.along(0, k)
            gather.across(1, k - 1)
            gather.across(0, k - 1)
        gather.across(1, DEPTH - 1)
        gather.across(0, DEPTH - 1)
        gather.along(2, 0)
        gather.last(0)
        swap.start()
        gather.last(1)
        gather.along(3, 0)
        saves[0].start()
        for j in range(width // edge):
            wo[pl.ds(j // 2 * edge, edge), pl.ds(j % 2 * half, half)] = wk[
                pl.ds(j * edge, edge), pl.ds(3 * half, half)
            ]
        saves[1].start()
        swap.wait()
        flat[...] = jnp.zeros_like(flat)
        for t in range(2):
            for d in range(DEPTH * PLANE):
                flat[t : t + 1, pl.ds(d * shard, shard)] = vecs[t, d, 0:1, pl.ds(0, shard)]

    @pl.when(lax.rem(i, steps) == 0)
    def _():
        bq, bv = flat[pl.ds(own, 1), pl.ds(0, half)], flat[pl.ds(own, 1), pl.ds(half, half)]
        bias = jnp.concatenate([bq, jnp.zeros_like(bq), bv], axis=1)
        qkv[...] = (nn(tok[...], wk[:, pl.ds(0, 3 * half)]) + bias).astype(BF)

    schedule = [
        (3, lambda: (gather.along(2, 1), gather.across(2, 0))),
        (5, lambda: (gather.along(3, 1), gather.across(3, 0))),
        (7, lambda: (gather.along(2, 2), gather.across(2, 1))),
        (9, lambda: (gather.along(3, 2), gather.across(3, 1))),
        (11, lambda: (gather.along(2, 3), gather.across(2, 2))),
        (13, lambda: (gather.along(3, 3), gather.across(3, 2))),
        (16, lambda: gather.across(2, 3)),
        (18, lambda: gather.across(3, 3)),
        (20, lambda: (gather.last(2), saves[2].start())),
    ]
    rows = pl.ds(pl.multiple_of(lax.rem(i, steps) * blk, blk), blk)
    stats = attend(
        qkv, ctx, hot[0, rows, :], cold[0], rows, half, lambda pair: play(schedule, pair)
    )
    lse[0, :, rows] = stats.T[: lse.shape[1]]

    @pl.when(lax.rem(i, steps) == steps - 1)
    def _():
        part[...] = nn(ctx[...], wo[...]).astype(BF)

    @pl.when(i == pl.num_programs(0) - 1)
    def _():
        gather.last(3)
        saves[3].start()
        gather.sent()
        for save in saves:
            save.wait()


def front(tok, hot, cold, mat, vec, rows, seq, blk=256):
    per, edge = mat.shape[0] // KINDS, mat.shape[-1]
    count, width = tok.shape
    half = width // 2
    stat_rows = -(-(half // HD) // 8) * 8
    chips = DEPTH * PLANE
    steps = seq // blk
    row = lambda shape: pl.BlockSpec(shape, lambda i: (i // steps,) + (0,) * (len(shape) - 1))
    hbm = pl.BlockSpec(memory_space=pl.ANY)
    weights = [(width, 2 * width), (half, width), (2, width, width), (2 * width, width)]
    return pl.pallas_call(
        partial(front_kernel, edge=edge, per=per, seq=seq, blk=blk, steps=steps),
        grid=(rows * steps,),
        in_specs=[
            row((seq, width)),
            row((1, seq, LANES)),
            row((1, seq, LANES)),
            once(mat.shape),
            once(vec.shape),
        ],
        out_specs=[
            row((seq, 3 * half)),
            row((seq, half)),
            row((1, stat_rows, seq)),
            row((seq, width)),
            once((8, chips * vec.shape[1])),
            *[hbm] * 4,
        ],
        out_shape=[
            jax.ShapeDtypeStruct((count, 3 * half), BF),
            jax.ShapeDtypeStruct((count, half), BF),
            jax.ShapeDtypeStruct((rows, stat_rows, seq), F32),
            jax.ShapeDtypeStruct((count, width), BF),
            jax.ShapeDtypeStruct((8, chips * vec.shape[1]), F32),
            *[jax.ShapeDtypeStruct(shape, BF) for shape in weights],
        ],
        scratch_shapes=[
            pltpu.VMEM(weights[0], BF),
            pltpu.VMEM(weights[2], BF),
            pltpu.VMEM(weights[3], BF),
            pltpu.VMEM((2, chips, VEC_ROWS, -(-vec.shape[1] // LANES) * LANES), F32),
            pltpu.VMEM(weights[1], BF),
            pltpu.SemaphoreType.DMA((4, 6, chips)),
            pltpu.SemaphoreType.DMA((4, GATHER_SLOTS)),
            pltpu.SemaphoreType.DMA((2,)),
            pltpu.SemaphoreType.DMA((4,)),
        ],
        compiler_params=params(collective_id=2, has_side_effects=True),
        name="front",
    )(tok, hot, cold, mat, vec)


def back_kernel(
    gattn, qkv, ctx, lse, wk, w_out, hot, cold, sums, up_sum, r1_grad, tok_all, g1_in, g2_in,
    input_grad, tot0, tot1, tot2, totv,
    tok, g0, g1, g2, gv, gqkv, gctx, centre, dk, dv, out_grad, bias_sums, part, got_part,
    *rest, edge, per, steps, row_count, blk, shard,
):
    i = pl.program_id(0)
    count, width = tok.shape
    half = width // 2
    seq = gctx.shape[0]
    compute = row_count * steps
    me = lax.axis_index("tensor")
    gots, (send_sem, recv_sem, part_sem, load_sem) = rest[:-4], rest[-4:]
    gots = [gots[c * 6 : (c + 1) * 6] for c in range(4)]

    def place0(d):
        return g0.at[d]

    def place1(d):
        return g1.at[lax.rem(d, 2), pl.ds(pl.multiple_of(d // 2 * edge, edge), edge)]

    def place2(d):
        return g2.at[pl.ds(pl.multiple_of(d * edge, edge), edge)]

    def place3(d):
        return gv.at[d]

    VEC, DOWN_W, UP_W, ATT = range(4)
    scatter = Scatter(
        [
            (place3, VEC_ROWS, VEC_ROWS, totv, gots[VEC]),
            (place2, edge // 2, edge, tot2, gots[DOWN_W]),
            (place1, edge // 2, edge, tot1, gots[UP_W]),
            (place0, edge, 2 * edge, tot0, gots[ATT]),
        ],
        send_sem,
        recv_sem,
    )
    far_first = [jnp.where(scatter.z < DEPTH // 2, DEPTH - 1 - k, k) for k in range(DEPTH)]
    loads = [
        pltpu.make_async_copy(src, dst, load_sem.at[n])
        for n, (src, dst) in enumerate(((g2_in, g2), (g1_in, g1), (tok_all, tok)))
    ]

    def swap(r):
        at = pl.ds(pl.multiple_of(r * seq, seq), seq)
        return pltpu.make_async_remote_copy(
            src_ref=part.at[at],
            dst_ref=got_part.at[at],
            send_sem=part_sem.at[0, r],
            recv_sem=part_sem.at[1, r],
            device_id={"tensor": 1 - me},
            device_id_type=MESH,
        )

    @pl.when(i == 0)
    def _():
        for load in loads:
            load.start()
        greet()

    def begin(c, load):
        loads[load].wait()
        for k in range(DEPTH):
            scatter.first(c, far_first[k])

    second = lambda c, k: (lambda: scatter.second(c, far_first[k]))
    third = lambda c, k: (lambda: scatter.third(c, far_first[k]))
    schedule = [
        (0, lambda: begin(DOWN_W, 0)),
        (1, lambda: begin(UP_W, 1)),
        (2, second(DOWN_W, 0)),
        (3, second(DOWN_W, 1)),
        (4, second(DOWN_W, 2)),
        (5, second(DOWN_W, 3)),
        (6, lambda: (third(DOWN_W, 0)(), second(UP_W, 0)())),
        (7, lambda: (third(DOWN_W, 1)(), second(UP_W, 1)())),
        (8, lambda: (third(DOWN_W, 2)(), second(UP_W, 2)())),
        (9, lambda: (third(DOWN_W, 3)(), second(UP_W, 3)())),
        (12, third(UP_W, 0)),
        (13, lambda: (third(UP_W, 1)(), scatter.first(ATT, 3))),
        (14, third(UP_W, 2)),
        (15, third(UP_W, 3)),
        (17, lambda: (scatter.last(DOWN_W), scatter.second(ATT, 3))),
        (19, lambda: scatter.last(UP_W)),
        (21, lambda: scatter.third(ATT, 3)),
    ]

    @pl.when((lax.rem(i, steps) == 0) & (i < compute))
    def _():
        context_grad(gattn, ctx, w_out, gctx, centre, half)
        dk[...] = jnp.zeros_like(dk)
        dv[...] = jnp.zeros_like(dv)

        @pl.when(i == 0)
        def _():
            out_grad[...] = jnp.zeros_like(out_grad)
            bias_sums[...] = jnp.zeros_like(bias_sums)

        out_grad[...] += tn(ctx[...], gattn[...])

        @pl.when(i == compute - steps)
        def _():
            for j in range(2 * PLANE):
                g0[3 * PLANE + j // 2, pl.ds(j % 2 * edge, edge)] = out_grad[
                    pl.ds(j // 2 * edge, edge), pl.ds(j % 2 * half, half)
                ].astype(BF)

    @pl.when(i < compute)
    def _():
        row = i // steps
        at = pl.multiple_of(lax.rem(i, steps) * blk, blk)
        rows = pl.ds(at, blk)
        there = pl.ds(pl.multiple_of(row * seq + at, blk), blk)
        bias_sums[0:1] += attend_back(
            qkv, gctx, lse.at[0], centre, hot[0, rows, :], cold[0], rows, half,
            gqkv.at[there, pl.ds(0, half)], dk, dv, lambda pair: play(schedule, pair),
        )

        @pl.when(lax.rem(i, steps) == steps - 1)
        def _():
            whole = pl.ds(pl.multiple_of(row * seq, seq), seq)
            gqkv[whole, pl.ds(half, half)] = dk[...].astype(BF)
            gqkv[whole, pl.ds(2 * half, half)] = dv[...].astype(BF)
            bias_sums[1:2] += fold(dv[...])
            part[whole] = nt(gqkv[whole], wk[:, pl.ds(0, 3 * half)]).astype(BF)
            swap(row).start()

    @pl.when(i == compute - 1)
    def _():
        loads[2].wait()
        flat = [bias_sums[0:1], bias_sums[1:2], up_sum[0:1]]
        flat += [sums[0:6, pl.ds(pl.multiple_of(me * half, half), half)][n : n + 1] for n in range(6)]
        flat = jnp.concatenate(flat, axis=1)
        sizes = sums[6:10, 0:LANES]
        for n in range(1, width // LANES):
            sizes = sizes + sums[6:10, pl.ds(n * LANES, LANES)]
        gv[...] = jnp.zeros_like(gv)
        for d in range(DEPTH * PLANE):
            gv[d, 0:1, pl.ds(0, shard)] = flat[:, d * shard : (d + 1) * shard]
            gv[d, 1:5, pl.ds(0, LANES)] = sizes
        for n in (2, 1, 0):
            grad = tn(tok[...], gqkv[:, pl.ds(n * half, half)]).astype(BF)
            for j in range(PLANE):
                g0[n * PLANE + j] = grad[2 * edge * j : 2 * edge * (j + 1)]
            scatter.first(ATT, n)
            if n == 2:
                for k in range(DEPTH):
                    scatter.first(VEC, k)
        for n in (2, 1, 0):
            scatter.second(ATT, n)
        for k in range(DEPTH):
            scatter.second(VEC, k)

    @pl.when(i >= steps)
    def _():
        chunk = i - steps
        row = chunk // steps
        pl.when(lax.rem(chunk, steps) == 0)(lambda: swap(row).wait())
        at = pl.ds(pl.multiple_of(chunk * blk, blk), blk)
        input_grad[...] = r1_grad[...] + part[at].astype(F32) + got_part[at].astype(F32)

    @pl.when(i == compute + steps - 1)
    def _():
        for n in (2, 1, 0):
            scatter.third(ATT, n)
        for k in range(DEPTH):
            scatter.third(VEC, k)
        scatter.last(ATT)
        scatter.last(VEC)
        for c in range(4):
            scatter.sent(c)


def back(gattn, qkv, ctx, lse, wk, w_out, hot, cold, sums, up_sum, r1_grad, tok, g1, g2, rows, seq, shard, blk=256):
    count, width = tok.shape
    half = width // 2
    edge = width // 8
    chips = DEPTH * PLANE
    steps = seq // blk
    compute = rows * steps
    row = lambda shape: pl.BlockSpec(
        shape, lambda i: (jnp.minimum(i // steps, rows - 1),) + (0,) * (len(shape) - 1)
    )
    late = pl.BlockSpec((blk, width), lambda i: (jnp.maximum(i - steps, 0), 0))
    hbm = pl.BlockSpec(memory_space=pl.ANY)
    wide = -(-shard // LANES) * LANES
    return pl.pallas_call(
        partial(back_kernel, edge=edge, per=8, steps=steps, row_count=rows, blk=blk, shard=shard),
        grid=(compute + steps,),
        in_specs=[
            row((seq, width)),
            row((seq, 3 * half)),
            row((seq, half)),
            row((1, lse.shape[1], seq)),
            once(wk.shape),
            once(w_out.shape),
            row((1, seq, LANES)),
            row((1, seq, LANES)),
            once(sums.shape),
            once(up_sum.shape),
            late,
            hbm,
            hbm,
            hbm,
        ],
        out_specs=[
            late,
            once((2 * edge, half)),
            once((edge, width)),
            once((edge, width)),
            once((VEC_ROWS, wide)),
        ],
        out_shape=[
            jax.ShapeDtypeStruct((count, width), F32),
            jax.ShapeDtypeStruct((2 * edge, half), F32),
            jax.ShapeDtypeStruct((edge, width), F32),
            jax.ShapeDtypeStruct((edge, width), F32),
            jax.ShapeDtypeStruct((VEC_ROWS, wide), F32),
        ],
        scratch_shapes=[
            pltpu.VMEM((count, width), BF),
            pltpu.VMEM((chips, 2 * edge, half), BF),
            pltpu.VMEM(g1.shape, BF),
            pltpu.VMEM(g2.shape, BF),
            pltpu.VMEM((chips, VEC_ROWS, wide), F32),
            pltpu.VMEM((count, 3 * half), BF),
            pltpu.VMEM((seq, half), BF),
            pltpu.VMEM((8, seq), F32),
            pltpu.VMEM((seq, half), F32),
            pltpu.VMEM((seq, half), F32),
            pltpu.VMEM((half, width), F32),
            pltpu.VMEM((8, half), F32),
            pltpu.VMEM((count, width), BF),
            pltpu.VMEM((count, width), BF),
            *landing(VEC_ROWS, VEC_ROWS, wide, F32),
            *landing(edge // 2, edge, width, BF),
            *landing(edge // 2, edge, width, BF),
            *landing(edge, 2 * edge, half, BF),
            pltpu.SemaphoreType.DMA((4, 6, DEPTH)),
            pltpu.SemaphoreType.DMA((4, 6, DEPTH)),
            pltpu.SemaphoreType.DMA((2, rows)),
            pltpu.SemaphoreType.DMA((3,)),
        ],
        compiler_params=params(collective_id=3, has_side_effects=True),
        name="back",
    )(gattn, qkv, ctx, lse, wk, w_out, hot, cold, sums, up_sum, r1_grad, tok, g1, g2)


def step_kernel(t0, t1, t2, master, left, right, root_l, root_r, grads, left_new, right_new, mat_new):
    kind = pl.program_id(0)
    per, edge = master.shape[0], master.shape[-1]

    def block(j, grad):
        low = grad.astype(BF)
        grads[j] = grad
        left_new[j] = DECAY * left[j] + (1.0 - DECAY) * nt(low, low)
        right_new[j] = DECAY * right[j] + (1.0 - DECAY) * tn(low, low)
        turned = nn(root_l[j].astype(BF), low).astype(BF)
        mat_new[j] = master[j] - STEP_RATE * nn(turned, root_r[j].astype(BF))

    @pl.when(kind == 0)
    def _():
        half = per // 2
        for j in range(per):
            block(j, t0[pl.ds(j // half * edge, edge), pl.ds(j % half * edge, edge)])

    for number, total in ((1, t1), (2, t2)):

        @pl.when(kind == number)
        def _():
            for j in range(per):
                block(j, total[:, pl.ds(j * edge, edge)])


def take_step(t0, t1, t2, master, left, right, root_l, root_r):
    per, edge = master.shape[0] // KINDS, master.shape[-1]
    blocks = pl.BlockSpec((per, edge, edge), lambda k: (k, 0, 0))
    return pl.pallas_call(
        step_kernel,
        grid=(KINDS,),
        in_specs=[once(t0.shape), once(t1.shape), once(t2.shape), *[blocks] * 5],
        out_specs=[blocks] * 4,
        out_shape=[jax.ShapeDtypeStruct(master.shape, F32)] * 4,
        compiler_params=params(),
        name="take_step",
    )(t0, t1, t2, master, left, right, root_l, root_r)


def far_weights(mat_master, vec_master, width):
    half = width // 2
    edge = mat_master.shape[-1]
    local = mat_master.astype(BF).reshape(KINDS, -1, edge, edge)
    blocks = lax.all_gather(local, "dp", axis=1, tiled=True)
    kind_count = blocks.shape[1]
    quarter = kind_count // 4
    grid_model = width // edge
    grid_half = half // edge
    grid_hidden = kind_count // grid_model
    w_project = (
        blocks[0, : 3 * quarter]
        .reshape(3, grid_model, grid_half, edge, edge)
        .transpose(1, 3, 0, 2, 4)
        .reshape(width, 3 * half)
    )
    w_out = unblock(blocks[0, 3 * quarter :], grid_half, grid_model)
    w_up = unblock(blocks[1], grid_model, grid_hidden).reshape(width, -1, width)
    w_down = unblock(blocks[2], grid_hidden, grid_model)
    shard = vec_master.shape[0]
    every = lax.all_gather(vec_master, ("dp", "tensor"), axis=0, tiled=True)
    flat = every.reshape(-1, 2, shard).transpose(1, 0, 2).reshape(2, 12 * half)
    return w_project, w_out, w_up.transpose(1, 0, 2), w_down, jnp.pad(flat, ((0, 6), (0, 0)))


def far_step(grads, state):
    grad_project, grad_out_weight, grad_up, grad_down, vec_local, sizes = grads
    mat_master, mat_left, mat_right, root_left, root_right = state
    edge = mat_master.shape[-1]
    width, half = grad_project.shape[0], grad_project.shape[1] // 3
    project_blocks = (
        grad_project.reshape(width // edge, edge, 3, half // edge, edge)
        .transpose(2, 0, 3, 1, 4)
        .reshape(-1, edge, edge)
    )
    attention_blocks = jnp.concatenate([project_blocks, to_blocks(grad_out_weight, edge)], axis=0)
    grad_up = grad_up.transpose(1, 0, 2).reshape(width, -1)
    owned = lax.psum_scatter(
        jnp.stack([attention_blocks, to_blocks(grad_up, edge), to_blocks(grad_down, edge)]),
        "dp",
        scatter_dimension=1,
        tiled=True,
    )
    vec_grads = lax.psum_scatter(vec_local, "dp", scatter_dimension=0, tiled=True)
    mat_grads = owned.astype(F32).reshape(-1, edge, edge)
    left_new = DECAY * mat_left + (1.0 - DECAY) * jnp.einsum("bij,bkj->bik", mat_grads, mat_grads)
    right_new = DECAY * mat_right + (1.0 - DECAY) * jnp.einsum("bji,bjk->bik", mat_grads, mat_grads)
    turned = jnp.einsum("bij,bjk->bik", root_left, mat_grads)
    turned = jnp.einsum("bij,bjk->bik", turned, root_right)
    mat_new = mat_master - STEP_RATE * turned
    return (mat_grads, left_new, right_new, mat_new), vec_grads, lax.psum(sizes, "dp")


def body(
    tokens,
    cotangent,
    pair_lengths,
    mat_master,
    mat_left,
    mat_right,
    root_left,
    root_right,
    vec_master,
    vec_second,
):
    width = tokens.shape[1]
    half = width // 2
    row_count, pair_count = pair_lengths.shape
    seq = tokens.shape[0] // row_count
    edge = mat_master.shape[-1]
    shard = vec_master.shape[0]
    own_index = lax.axis_index("tensor")
    near = lax.axis_size("dp") == DEPTH * PLANE and mat_master.shape[0] == KINDS * width // edge

    place = lax.broadcasted_iota(jnp.int32, (row_count, seq, pair_count), 1)
    upto = jnp.tril(jnp.ones((pair_count, pair_count), jnp.int32))
    ends = jnp.sum(pair_lengths[:, None, :] * upto[None], axis=-1)
    pairs = jnp.sum((place >= ends[:, None, :]).astype(jnp.int32), axis=-1)
    ids = lax.broadcasted_iota(jnp.int32, (row_count, seq, LANES), 2)
    same = pairs[:, :, None] == ids
    hot = same.astype(BF)
    cold = jnp.where(same & (ids < pair_count), 0.0, -BIG).astype(BF)
    keep = (pairs < pair_count).astype(F32).reshape(-1)
    valid = jnp.broadcast_to(keep[:, None], (keep.shape[0], LANES))
    state = (mat_master, mat_left, mat_right, root_left, root_right)

    if near:
        qkv, ctx, lse, part, flat, wk, w_out, w_up, w_down = front(
            tokens, hot, cold, mat_master, vec_master[None], row_count, seq
        )
    else:
        w_project, w_out, w_up, w_down, flat = far_weights(mat_master, vec_master, width)
        own = lax.dynamic_slice_in_dim(flat, own_index, 1)
        bias = jnp.concatenate([own[:, :half], jnp.zeros((1, half), F32), own[:, half : 2 * half]], axis=1)
        qkv, ctx, lse, part = attn_fwd(tokens, w_project, w_out, bias, hot, cold, row_count, seq)
    block_out, gr1, gattn, grad_up, grad_down, sums, up_sum = feed(
        tokens, cotangent, valid, part, w_up, w_down, flat
    )
    if near:
        input_grad, tot0, tot1, tot2, totv = back(
            gattn, qkv, ctx, lse, wk, w_out, hot, cold, sums, up_sum, gr1, tokens,
            grad_up, grad_down, row_count, seq, shard,
        )
        mats = take_step(tot0, tot1, tot2, *state)
        vec_grads = totv[0, :shard]
        sizes = jnp.sum(totv[1:5, :LANES], axis=1)
    else:
        gqkv, bias_sums, part_in = attn_bwd(
            gattn, qkv, ctx, lse, w_project, w_out, hot, cold, row_count, seq
        )
        swap = [(0, 1), (1, 0)]
        input_grad = gr1 + part_in.astype(F32) + lax.ppermute(part_in, "tensor", swap).astype(F32)
        bias_pair = jnp.sum(bias_sums, axis=0)
        shared_sums = lax.dynamic_slice_in_dim(sums[:6], own_index * half, half, axis=1)
        vec_local = jnp.concatenate([bias_pair[:2].reshape(-1), up_sum[0], shared_sums.reshape(-1)])
        sizes = jnp.sum(sums[6:10], axis=1)
        grads = (tn(tokens, gqkv).astype(BF), tn(ctx, gattn).astype(BF), grad_up, grad_down)
        mats, vec_grads, sizes = far_step((*grads, vec_local, sizes), state)
    stream_rms = jnp.sqrt(sizes[:3] / (sizes[3] * width / LANES))
    second_new = DECAY * vec_second + (1.0 - DECAY) * vec_grads * vec_grads
    vec_new = vec_master - VEC_RATE * vec_grads / (jnp.sqrt(second_new) + VEC_EPS)
    return (block_out, input_grad, *mats, vec_grads, second_new, vec_new, stream_rms)


def solution(mesh):
    blocks = P(("dp", "tensor"), None, None)
    rows = P("dp", None)
    entries = P(("dp", "tensor"))
    return jax.shard_map(
        body,
        mesh=mesh,
        in_specs=(rows, rows, rows, *[blocks] * 5, entries, entries),
        out_specs=(rows, rows, *[blocks] * 4, entries, entries, entries, P()),
        check_vma=False,
    )
```

time: 415 us -> 306 us (0.74)
  Pallas kernels: 322 us -> 287 us
  matrix products: 30.6 us -> 0 us
  local copies, waits for them, and re-layouts: 37.1 us -> 10.5 us
  other arithmetic: 18.6 us -> 5.13 us
    pallas_call x5 -> x4, Pallas kernels: 322 us -> 287 us  [the longest x1 126 us: back(): pl.pallas_call(partial(back_kernel, edge=edge, per=8, steps=steps, row_co...]
    dot_general x4 -> x0, matrix products: 30.6 us -> none  [tn(): lax.dot_general(a, b, (((0,), (0,)), ((), ())), preferred_element_type=F32)]
    reshape x11 -> x0, local copies, waits for them, and re-layouts: 11.4 us -> none  [the longest x1 3.29 us: near_step(): grad_project.reshape(PLANE, 2 * edge, 3, half).transpose(2, 0, 1, 3)]
    add x1 -> x0, other arithmetic: 7.4 us -> none  [body(): gr1 + part_in.astype(F32)]
    convert_element_type x2 -> x0, local copies, waits for them, and re-layouts: 5.04 us -> none  [the longest x1 2.83 us: body(): grad_up = tn(hid, gpre).astype(BF)]
    concatenate x6 -> x0, other arithmetic: 4.65 us -> none  [the longest x1 3.3 us: near_step(): jnp.concatenate([project.reshape(3 * PLANE, 2 * edge, half), out.reshape(...]
    unnamed x47 -> x13, local copies, waits for them, and re-layouts: 9.36 us -> 6.64 us
  transfers between devices with their start and end apart: 1 -> 0, of which waited for: 0 -> 0; matrix products, arithmetic and copies ran while one was open for 13% -> 0% of each run, Pallas kernels for 23% -> 0%
where the time goes in v3:
time: 306 us; the launch traced here: 305 us
  Pallas kernels  287 us (94%)
  local copies, waits for them, and re-layouts  10.5 us (3%)
  other arithmetic  5.13 us (2%)
    pallas_call x1, Pallas kernels, back(): pl.pallas_call(partial(back_kernel, edge=edge, per=8, steps=steps, row_co...  126 us
    pallas_call x1, Pallas kernels, front(): pl.pallas_call(partial(front_kernel, edge=edge, per=per, seq=seq, blk=blk...  84.7 us
    pallas_call x1, Pallas kernels, feed(): pl.pallas_call(partial(feed_kernel, tiles=tiles, blk=blk), grid=(tiles +...  68.8 us
    pallas_call x1, Pallas kernels, take_step(): pl.pallas_call(step_kernel, grid=(KINDS,), in_specs=[once(t0.shape), once...  7.99 us
    unnamed x13, local copies, waits for them, and re-layouts  6.64 us

profile of v3, /device:TPU:0, one launch (start us, length us, event | category | flops | bytes accessed | tf_op | source)
XLA Modules:
  0.0 304.7 jit_solution(12876105191280769929)
XLA Ops:
  0.7 1.2 broadcast_in_dim.32.vec
  1.9 0.8 multiply_reduce_fusion
  2.7 0.1 convert_reduce_fusion
  2.9 1.1 select_convert_fusion.cold
  4.0 1.1 fusion.1.hot
  5.1 1.3 broadcast_in_dim.29.valid0.valid1
  6.4 84.7 %front.1 = (bf16[2048,1152]{1,0:T(8,128)(2,1)}, bf16[2048,384]{1,0:T(8,128)(2,1)}, f32[2,8,1024]{2,1,0:T(8,128)}, bf16[2048,768]{1,0:T(8,128)(2,1)}, f32[8,4608]...) custom-call(bf16[2048,768]{1,0:T(8,128)(2,1)} %tok_all.1, ...), custom_call_target="tpu_custom_call" | custom-call | tf_op jit(solution)/shard_map/front/pallas_call | solution.py:861
  91.1 68.8 %feed.1 = (bf16[2048,768]{1,0:T(8,128)(2,1)}, f32[2048,768]{1,0:T(8,128)}, bf16[2048,768]{1,0:T(8,128)(2,1)}, bf16[2,768,768]{2,1,0:T(8,128)(2,1)}, bf16[1536,76...) custom-call(bf16[2048,768]{1,0:T(8,128)(2,1)} %tok_all.1, bf16[2048,768]{1,0:T(8,128)(2,1)} %cot.1, ...), custom_call_target="tpu_custom_call" | custom-call | tf_op jit(solution)/shard_map/feed/pallas_call | solution.py:419
  159.9 0.0 copy-start.2
  159.9 0.0 copy-start.4
  160.0 125.9 %back.1 = (f32[2048,768]{1,0:T(8,128)}, f32[192,384]{1,0:T(8,128)}, f32[96,768]{1,0:T(8,128)}, f32[96,768]{1,0:T(8,128)}, f32[8,384]{1,0:T(8,128)}) custom-call(bf16[2048,768]{1,0:T(8,128)(2,1)} %get-tuple-element.40.gattn, bf16[2048,1152]{1,0:T(8,128)(2,1)} %get-tuple-element.41.qkv, bf16[2048,384]{1,0:T(8,128)(2,1)} %get-tuple-element.42.ctx, ...), custom_call_target="tpu_custom_call" | custom-call | tf_op jit(solution)/shard_map/back/pallas_call | solution.py:1090
  285.9 0.8 slice_reduce_fusion
  286.7 0.6 slice.15
  287.9 0.7 slice_reduce_fusion.1
  288.7 0.0 copy-start.3
  288.7 0.5 divide_sqrt_fusion
  289.2 0.0 copy-done.2
  289.2 0.0 copy-done.4
  289.2 0.6 divide_subtract_fusion
  289.8 0.0 copy-start.1
  289.8 8.0 %take_step.1 = (f32[24,96,96]{2,1,0:T(8,128)}, f32[24,96,96]{2,1,0:T(8,128)}, f32[24,96,96]{2,1,0:T(8,128)}, f32[24,96,96]{2,1,0:T(8,128)}) custom-call(f32[192,384]{1,0:T(8,128)} %get-tuple-element.52.t0, f32[96,768]{1,0:T(8,128)} %get-tuple-element.53.t1, f32[96,768]{1,0:T(8,128)} %get-tuple-element.54.t2, f32[24,96,96]{2,1,0:T(8,128)} %master.1, ...), custom_call_target="tpu_custom_call" | custom-call | tf_op jit(solution)/shard_map/take_step/pallas_call | solution.py:1181
  297.8 0.0 copy-done.3
  297.8 0.0 copy-done.1
  297.8 0.0 copy-start
  297.8 1.7 copy.25
  299.5 2.2 copy-done
  301.7 2.7 copy.26
  (4 shorter events, 0.0 us)
Async XLA Ops:
  159.9 129.3 %copy-start.2 = (f32[288]{0:T(512)S(1)}, f32[288]{0:T(512)}, u32[]{:S(2)}) copy-start(f32[288]{0:T(512)} %param.18) | copy-start | bytes 3460
  159.9 129.3 %copy-start.4 = (f32[288]{0:T(512)S(1)}, f32[288]{0:T(512)}, u32[]{:S(2)}) copy-start(f32[288]{0:T(512)} %param.19) | copy-start | bytes 3460
  288.7 9.1 %copy-start.3 = (f32[288]{0:T(512)}, f32[288]{0:T(512)S(1)}, u32[]{:S(2)}) copy-start(f32[288]{0:T(512)S(1)} %slice_reduce_fusion.1) | copy-start | bytes 3460
  289.8 8.0 %copy-start.1 = (bf16[2048,768]{1,0:T(8,128)(2,1)S(1)}, bf16[2048,768]{1,0:T(8,128)(2,1)}, u32[]{:S(2)}) copy-start(bf16[2048,768]{1,0:T(8,128)(2,1)} %get-tuple-element.72) | copy-start | bytes 9437188
  297.8 3.9 %copy-start = (f32[2048,768]{1,0:T(8,128)S(1)}, f32[2048,768]{1,0:T(8,128)}, u32[]{:S(2)}) copy-start(f32[2048,768]{1,0:T(8,128)} %get-tuple-element.73) | copy-start | bytes 18874372
